TPU v7x, 128 devices: a whole 4x4x4 slice. The times are simulated.
128 devices in a mesh: frame: 8 (over x, z_hi), pos: 16 (over y, z_lo, core).
Axes of the slice: x: 4, y: 4, z: 4 (z_hi: 2, z_lo: 2; z = z_hi * 2 + z_lo), core: 2. Of those that a mesh axis runs over, the one named last changes fastest.
Arguments:
- tokens: bfloat16 [64, 1024, 1152], P('frame', 'pos'), may hold values from -6 to 6
- frame_valid: int32 [64], replicated, may hold values from 0 to 1, as said below
- text: bfloat16 [300, 1152], replicated, may hold values from -6 to 6
- modulation: float32 [6, 1152], replicated, may hold values from -4 to 4
- qk_gains: float32 [4, 72], replicated, may hold values from 0.8 to 4.5, as said below
- spatial_qkv: bfloat16 [1152, 3456], replicated
- spatial_out: bfloat16 [1152, 1152], replicated, may hold values from -0.1875 to 0.1875
- block_weights: bfloat16 [1152, 6912], P('frame')
- cross_kv: bfloat16 [1152, 2, 1152], P(None, None, 'pos'), may hold values from -0.1875 to 0.1875
Outputs:
- mixed: bfloat16 [64, 1024, 1152], P('frame', 'pos')
Inputs may be any that keep to these rules, and one draw needn't show every extreme that they name: `frame_valid`: 1 for a leading run of frames and 0 after it; frame 0 is always 1, the last frame always 0, and at least 16 frames are 1. `qk_gains`: positive.
All inputs are finite; a program needn't handle non-finite values.
Results may differ from a plain program's by a relative error of at most 0.02.
Values may be sent and summed in bfloat16 or wider, within the bound.
No kernel may reach another device: no remote copies, remote signals or barrier semaphores. Data moves between devices by JAX's collectives and lax.ppermute only.
A program may use at most 320 MiB of HBM per device.

v0:
```python
import functools
import jax
import jax.numpy as jnp
from jax import lax
from jax.experimental import pallas as pl
from jax.experimental.pallas import tpu as pltpu

D = 1152
HD = 72
HEADS = 16
WIN = 256
TEXT = 300
TPAD = 304
SHARD = 144
HALF = 80
SAFE = 96.0
BF = jnp.bfloat16
F32 = jnp.float32


def dot(a, b):
    return jnp.dot(a, b, preferred_element_type=F32)


def indicators():
    feature = lax.broadcasted_iota(jnp.int32, (D, 128), 0)
    low = lax.broadcasted_iota(jnp.int32, (D, 128), 1) * HD
    gather = ((feature >= low) & (feature < low + HD)).astype(F32).astype(BF)
    feature = lax.broadcasted_iota(jnp.int32, (256, D), 1)
    low = lax.rem(lax.broadcasted_iota(jnp.int32, (256, D), 0), 128) * HD
    spread = ((feature >= low) & (feature < low + HD)).astype(F32).astype(BF)
    return gather, spread


def norm_rows(x, shift, scale):
    mean = jnp.mean(x, -1, keepdims=True)
    centred = x - mean
    r = lax.rsqrt(jnp.mean(centred * centred, -1, keepdims=True) + 1e-6)
    return (centred * r * (1.0 + scale) + shift).astype(BF)


def head_norm_rows(u, gather, spread, gain):
    total = dot((u * u).astype(BF), gather)
    r = lax.rsqrt(total * (1.0 / HD) + 1e-6)
    high = r.astype(BF)
    low = (r - high.astype(F32)).astype(BF)
    return (u * dot(jnp.concatenate([high, low], -1), spread) * gain).astype(BF)


def window_of(h):
    start = jnp.minimum((h * HD) // 128 * 128, D - WIN)
    return pl.multiple_of(start, 128), h * HD - start


def head_rows(h):
    return pl.ds(pl.multiple_of(h * HD, 8), HD)


def query_of(qt, h, normed):
    start, off = window_of(h)
    win = pl.ds(start, WIN)
    row = lax.broadcasted_iota(jnp.int32, (WIN, 1), 0)
    mine = (row >= off) & (row < off + HD)
    own = qt[head_rows(h), :]
    if not normed:
        return jnp.where(mine, qt[win, :], 0.0).astype(BF)
    r = lax.rsqrt(jnp.sum(own * own, 0, keepdims=True) * (1.0 / HD) + 1e-6)
    return (jnp.where(mine, qt[win, :], 0.0) * r).astype(BF)


def softmax(s, shifted):
    if shifted:
        s = s - jnp.max(s, 0, keepdims=True)
    return jnp.exp2(s).astype(BF)


def values_of(vt, h, cols):
    v = vt[head_rows(h), cols].astype(BF)
    return jnp.concatenate([v, jnp.ones((8, v.shape[1]), BF)], 0)


def loop(n, body):
    def step(i, carry):
        body(i)
        return carry

    lax.fori_loop(0, n, step, 0)


def guarded(gain, run):
    bound = jnp.max(gain[...]) * HD

    @pl.when(bound <= SAFE)
    def _():
        run(False)

    @pl.when(bound > SAFE)
    def _():
        run(True)


def spatial_kernel(own, other, wqkv, wout, mod, gain, out, xin, k, qt, vt, at, *, rows):
    gather, spread = indicators()
    shift, scale, gate = mod[0:1, :], mod[1:2, :], mod[2:3, :]
    R = 256
    for b in range(rows // R):
        sl = pl.ds(b * R, R)
        xin[sl, :] = norm_rows(own[sl, :].astype(F32), shift, scale)
        xin[pl.ds(rows + b * R, R), :] = norm_rows(other[sl, :].astype(F32), shift, scale)
    for b in range(rows // R):
        sl = pl.ds(b * R, R)
        qt[:, sl] = dot(xin[sl, :], wqkv[:, 0:D]).T
    for b in range(2 * rows // R):
        sl = pl.ds(b * R, R)
        k[sl, :] = head_norm_rows(dot(xin[sl, :], wqkv[:, D:2 * D]), gather, spread, gain[...])
        vt[:, sl] = dot(xin[sl, :], wqkv[:, 2 * D:]).T

    def run(shifted):
        def pair(i):
            for h in (2 * i, 2 * i + 1):
                start, _ = window_of(h)
                q = query_of(qt, h, True)
                p = softmax(dot(k[:, pl.ds(start, WIN)], q), shifted)
                o = dot(values_of(vt, h, slice(None)), p)
                at[head_rows(h), :] = o[:HD] * (1.0 / o[HD:HD + 1])

        loop(HEADS // 2, pair)

    guarded(gain, run)
    for b in range(rows // R):
        sl = pl.ds(b * R, R)
        proj = dot(at[:, sl].T.astype(BF), wout[...])
        out[sl, :] = (own[sl, :].astype(F32) + gate * proj).astype(BF)


VMEM = pl.BlockSpec(memory_space=pltpu.VMEM)
PARAMS = pltpu.CompilerParams(vmem_limit_bytes=60 * 2**20)


def spatial(own, other, wqkv, wout, mod, gain):
    rows = own.shape[0]
    return pl.pallas_call(
        functools.partial(spatial_kernel, rows=rows),
        out_shape=jax.ShapeDtypeStruct((rows, D), BF),
        in_specs=[VMEM] * 6,
        out_specs=VMEM,
        scratch_shapes=[
            pltpu.VMEM((2 * rows, D), BF),
            pltpu.VMEM((2 * rows, D), BF),
            pltpu.VMEM((D, rows), F32),
            pltpu.VMEM((D, 2 * rows), F32),
            pltpu.VMEM((D, rows), F32),
        ],
        compiler_params=PARAMS,
        cost_estimate=pl.CostEstimate(flops=3 * 10**10, bytes_accessed=2 * 10**7, transcendentals=0),
        name="spatial",
    )(own, other, wqkv, wout, mod, gain)


def piece_copies(place, gathered, weight, sems):
    z = place[0]
    width = gathered.shape[3]
    parts = weight.shape[1] // width
    copies = []
    for x in range(4):
        for y in range(parts):
            for core in range(2):
                low, count = (0, HALF) if core == 0 else (HALF - 64, 64)
                for dz in range(2):
                    shard = 2 * x + (z if dz == 0 else 1 - z)
                    row = pl.multiple_of(shard * SHARD + core * HALF, 16)
                    dst = weight.at[pl.ds(row, count), pl.ds(y * width, width)]
                    src = gathered.at[(x * parts + y) * 2 + core, dz, pl.ds(low, count), :]
                    copies.append(pltpu.make_async_copy(src, dst, sems.at[len(copies)]))
    return copies


def ordered(rows, source_of):
    to = lax.broadcasted_iota(jnp.int32, (rows, rows), 0)
    source = lax.broadcasted_iota(jnp.int32, (rows, rows), 1)
    return (source == source_of(to)).astype(F32).astype(BF)


def temporal_kernel(place, gathered, x, valid, mod, gain, out, w, xp, xin, k, qt, vt, at, sems, *, rows, frames):
    copies = piece_copies(place, gathered, w, sems)
    for copy in copies:
        copy.start()
    gather, spread = indicators()
    places = rows // frames
    shift, scale, gate = mod[3:4, :], mod[4:5, :], mod[5:6, :]
    R = 256
    order = ordered(rows, lambda to: lax.rem(to, frames) * places + to // frames)
    for b in range(rows // R):
        sl = pl.ds(b * R, R)
        moved = dot(order[b * R:(b + 1) * R, :], x[...])
        xp[sl, :] = moved.astype(BF)
        xin[sl, :] = norm_rows(moved, shift, scale)
    for copy in copies:
        copy.wait()
    for b in range(rows // R):
        sl = pl.ds(b * R, R)
        qt[:, sl] = dot(xin[sl, :], w[:, 0:D]).T
        k[sl, :] = head_norm_rows(dot(xin[sl, :], w[:, D:2 * D]), gather, spread, gain[...])
        vt[:, sl] = dot(xin[sl, :], w[:, 2 * D:3 * D]).T

    key = lax.broadcasted_iota(jnp.int32, (R, R), 0) // frames
    query = lax.broadcasted_iota(jnp.int32, (R, R), 1) // frames
    bias = jnp.where(key == query, 0.0, -1e30) + valid[...]

    def run(shifted):
        def pair(i):
            for h in (2 * i, 2 * i + 1):
                start, _ = window_of(h)
                q = query_of(qt, h, True)
                for b in range(rows // R):
                    sl = pl.ds(b * R, R)
                    s = dot(k[sl, pl.ds(start, WIN)], q[:, b * R:(b + 1) * R]) + bias
                    o = dot(values_of(vt, h, sl), softmax(s, shifted))
                    at[head_rows(h), sl] = o[:HD] * (1.0 / o[HD:HD + 1])

        loop(HEADS // 2, pair)

    guarded(gain, run)
    for b in range(rows // R):
        sl = pl.ds(b * R, R)
        proj = dot(at[:, sl].T.astype(BF), w[:, 3 * D:])
        xin[sl, :] = (xp[sl, :].astype(F32) + gate * proj).astype(BF)
    groups = frames // 8

    def source_of(to):
        place, frame = lax.rem(to, places), to // places
        return place * frames + lax.rem(frame, 8) * groups + frame // 8

    order = ordered(rows, source_of)
    for b in range(rows // R):
        out[pl.ds(b * R, R), :] = dot(order[b * R:(b + 1) * R, :], xin[...]).astype(BF)


def temporal(place, gathered, x, valid, mod, gain):
    rows = x.shape[0]
    hbm = pl.BlockSpec(memory_space=pl.ANY)
    return pl.pallas_call(
        functools.partial(temporal_kernel, rows=rows, frames=64),
        out_shape=jax.ShapeDtypeStruct((rows, D), BF),
        in_specs=[pl.BlockSpec(memory_space=pltpu.SMEM)] + [hbm] + [VMEM] * 4,
        out_specs=VMEM,
        scratch_shapes=[
            pltpu.VMEM((D, 4 * D), BF),
            pltpu.VMEM((rows, D), BF),
            pltpu.VMEM((rows, D), BF),
            pltpu.VMEM((rows, D), BF),
            pltpu.VMEM((D, rows), F32),
            pltpu.VMEM((D, rows), F32),
            pltpu.VMEM((D, rows), F32),
            pltpu.SemaphoreType.DMA((64,)),
        ],
        compiler_params=PARAMS,
        cost_estimate=pl.CostEstimate(flops=2 * 10**10, bytes_accessed=2 * 10**7, transcendentals=0),
        name="temporal",
    )(place, gathered, x, valid, mod, gain)


def cross_kernel(place, gathered, x, tk, tvt, out, w, qt, at, sems):
    copies = piece_copies(place, gathered, w, sems)
    for copy in copies:
        copy.start()
    rows = x.shape[0]
    R = 256
    for copy in copies:
        copy.wait()
    for b in range(rows // R):
        sl = pl.ds(b * R, R)
        cq = dot(x[sl, :], w[:, :D]).astype(BF).astype(F32) * (HD ** -0.5 * 1.4426950408889634)
        qt[:, sl] = cq.T
    lane = lax.broadcasted_iota(jnp.int32, (8, TPAD), 1)
    ones = (lane < TEXT).astype(F32).astype(BF)

    def pair(i):
        for h in (2 * i, 2 * i + 1):
            start, _ = window_of(h)
            q = query_of(qt, h, False)
            p = softmax(dot(tk[:, pl.ds(start, WIN)], q), True)
            v = jnp.concatenate([tvt[head_rows(h), :].astype(BF), ones], 0)
            o = dot(v, p)
            at[head_rows(h), :] = o[:HD] * (1.0 / o[HD:HD + 1])

    loop(HEADS // 2, pair)
    for b in range(rows // R):
        sl = pl.ds(b * R, R)
        mixed = x[sl, :].astype(F32) + dot(at[:, sl].T.astype(BF), w[:, D:])
        for g in range(R // 64):
            for f in range(8):
                low = g * 64 + f * 8
                out[f, pl.ds((b * (R // 64) + g) * 8, 8), :] = mixed[low:low + 8, :].astype(BF)


def cross(place, gathered, x, tk, tvt):
    rows = x.shape[0]
    hbm = pl.BlockSpec(memory_space=pl.ANY)
    return pl.pallas_call(
        cross_kernel,
        out_shape=jax.ShapeDtypeStruct((8, rows // 8, D), BF),
        in_specs=[pl.BlockSpec(memory_space=pltpu.SMEM)] + [hbm] + [VMEM] * 3,
        out_specs=VMEM,
        scratch_shapes=[
            pltpu.VMEM((D, 2 * D), BF),
            pltpu.VMEM((D, rows), F32),
            pltpu.VMEM((D, rows), F32),
            pltpu.SemaphoreType.DMA((64,)),
        ],
        compiler_params=PARAMS,
        cost_estimate=pl.CostEstimate(flops=2 * 10**10, bytes_accessed=2 * 10**7, transcendentals=0),
        name="cross",
    )(place, gathered, x, tk, tvt)


import numpy as np
from jax.sharding import Mesh, PartitionSpec as P

XZ = ("x", "zh")
YZ = ("y", "zl")
RIGHT = [(i, (i + 1) % 4) for i in range(4)]
LEFT = [(i, (i + 3) % 4) for i in range(4)]
SWAP = [(0, 1), (1, 0)]
ACROSS = [(0, 3), (3, 0), (1, 2), (2, 1)]
bar = lax.optimization_barrier


def gains(gain_q, gain_k):
    return jnp.tile(gain_q * gain_k * (HD ** -0.5 * 1.4426950408889634), HEADS).reshape(1, D)


def across(v):
    return lax.ppermute(v, ("zh", "zl"), ACROSS)


def swap(v):
    return lax.ppermute(v, "c", SWAP)


def pos_quad(local, swapped):
    def both(v, axis, other):
        first = lax.axis_index(axis) == 0
        return jnp.concatenate([jnp.where(first, v, other), jnp.where(first, other, v)], 1)

    pair = both(local, "c", swapped)
    return both(pair, "zl", lax.ppermute(pair, "zl", SWAP))


def along_y(quad):
    return quad, lax.ppermute(quad, "y", RIGHT), lax.ppermute(quad, "y", [(i, (i + 2) % 4) for i in range(4)]), lax.ppermute(quad, "y", LEFT)


def in_order(steps):
    y = lax.axis_index("y")
    steps = jnp.stack(steps)
    return jnp.concatenate([lax.dynamic_index_in_dim(steps, lax.rem(y - i + 4, 4), 0, keepdims=False) for i in range(4)], 1)


def per_device(tokens, frame_valid, text, modulation, qk_gains, spatial_qkv, spatial_out, block_weights, cross_kv):
    core, y = lax.axis_index("c"), lax.axis_index("y")
    local = jnp.dot(text, cross_kv.reshape(D, 2 * HD), preferred_element_type=F32).astype(BF)
    swapped = swap(local)
    own = lax.all_to_all(tokens, YZ, 0, 0, tiled=True).reshape(-1, D)
    w1 = lax.dynamic_slice(block_weights, (64 * core, D * y), (HALF, D))
    w1, swapped = bar((w1, swapped))
    z1 = across(w1)
    both1 = jnp.stack([w1, z1])
    w2 = lax.dynamic_slice(block_weights, (64 * core, 4 * D), (HALF, 2 * D))
    w2, both1 = bar((w2, both1))
    gathered1 = lax.all_gather(both1, ("x", "y", "c"), axis=0)
    both2 = jnp.stack([w2, across(w2)])
    quad = pos_quad(local, swapped)
    gain_s = gains(qk_gains[0], qk_gains[1])
    gain_t = gains(qk_gains[2], qk_gains[3])
    seen = jnp.where(frame_valid.reshape(8, 8).T.reshape(64) > 0, 0.0, -1e30)
    valid = jnp.tile(seen, 4).reshape(256, 1).astype(F32)
    place = jnp.stack([lax.axis_index("zh"), core]).astype(jnp.int32)
    own, both2, quad, gain_s, gain_t, valid, place = bar((own, both2, quad, gain_s, gain_t, valid, place))

    other = swap(own)
    steps = along_y(quad)
    after_spatial = spatial(own, other, spatial_qkv, spatial_out, modulation, gain_s)
    after_spatial, steps = bar((after_spatial, steps))

    rows = lax.all_to_all(after_spatial.reshape(64, 8, D), YZ + XZ, 0, 0, tiled=True).reshape(-1, D)
    every = in_order(steps).reshape(TEXT, HEADS, 2, HD)
    tk = jnp.pad(every[:, :, 0].reshape(TEXT, D), ((0, TPAD - TEXT), (0, 0)), mode="edge")
    tvt = jnp.pad(every[:, :, 1].reshape(TEXT, D).T, ((0, 0), (0, TPAD - TEXT))).astype(F32)
    _, both2 = bar((rows, both2))
    gathered2 = lax.all_gather(both2, ("x", "c"), axis=0)
    after_temporal = temporal(place, gathered1, rows, valid, modulation, gain_t)

    back = lax.all_to_all(after_temporal.reshape(8, 64, D), XZ, 0, 0, tiled=True).reshape(-1, D)
    return cross(place, gathered2, back, tk, tvt)


def solution(mesh):
    fine = Mesh(np.asarray(mesh.devices).reshape(4, 2, 4, 2, 2), ("x", "zh", "y", "zl", "c"))
    pos = ("y", "zl", "c")
    placed = (P(XZ, pos, None), P(), P(), P(), P(), P(), P(XZ, None), P(None, None, pos))
    placed = placed[:6] + (P(),) + placed[6:]
    return jax.shard_map(per_device, mesh=fine, in_specs=placed, out_specs=P(XZ, pos, None), check_vma=False)
```

profile of v0, /device:TPU:8, one launch (start us, length us, event | category | flops | bytes accessed | tf_op | source)
XLA Modules:
  0.0 191.8 jit_solution(16493860037160105928)
XLA Ops:
  6.5 1.1 copy-done
  7.6 1.4 convolution_convert_fusion
  9.1 0.9 dynamic_slice.20
  10.4 4.0 %collective-permute-start.1 = (bf16[80,1152]{1,0:T(8,128)(2,1)S(1)}, bf16[80,1152]{1,0:T(8,128)(2,1)S(1)}, u32[]{:S(2)}, u32[]{:S(2)}) collective-permute-start(bf16[80,1152]{1,0:T(8,128)(2,1)S(1)} %dynamic_slice.20), channel_id=1, source_target_pairs={{0,18},{18,0},{2,16},{16,2},{1,19},{19,1},{3,17},{17,3},{4,22},{22... | collective-permute-start | bytes 552968 | tf_op jit(solution)/shard_map/ppermute | solution.py:334
  14.5 1.0 constant_dynamic-slice_fusion.4
  15.5 4.0 %collective-permute-done.1 = bf16[80,1152]{1,0:T(8,128)(2,1)S(1)} collective-permute-done((bf16[80,1152]{1,0:T(8,128)(2,1)S(1)}, bf16[80,1152]{1,0:T(8,128)(2,1)S(1)}, u32[]{:S(2)}, u32[]{:S(2)}) %collective-permute-start.1) | collective-permute-done | bytes 184352 | tf_op jit(solution)/shard_map/ppermute | solution.py:334
  20.3 5.0 %all-to-all-start = ((bf16[8,64,1152]{2,1,0:T(8,128)(2,1)}), bf16[8,64,1152]{2,1,0:T(8,128)(2,1)S(1)}, u32[]{:S(2)}, u32[]{:S(2)}) async-start(bf16[8,64,1152]{2,1,0:T(8,128)(2,1)} %param.9), calls=%async_computation | async-start | bytes 2359296 | tf_op jit(solution)/shard_map/all_to_all | solution.py:364
  25.4 1.5 collective-permute-start.3
  26.9 2.9 %collective-permute-start.2 = (bf16[80,2304]{1,0:T(8,128)(2,1)S(1)}, bf16[80,2304]{1,0:T(8,128)(2,1)S(1)}, u32[]{:S(2)}, u32[]{:S(2)}) collective-permute-start(bf16[80,2304]{1,0:T(8,128)(2,1)S(1)} %constant_dynamic-slice_fusion.4), channel_id=1, source_target_pairs={{0,18},{18,0},{2,16},{16,2},{1,19},{19,1},{3,17},{17,3},{4,22},{22... | collective-permute-start | bytes 1105928 | tf_op jit(solution)/shard_map/ppermute | solution.py:334
  32.2 12.1 %collective-permute-done.3 = bf16[300,288]{0,1:T(8,128)(2,1)S(1)} collective-permute-done((bf16[300,288]{0,1:T(8,128)(2,1)S(1)}, bf16[300,288]{0,1:T(8,128)(2,1)S(1)}, u32[]{:S(2)}, u32[]{:S(2)}) %collective-permute-start.3) | collective-permute-done | bytes 172832 | tf_op jit(solution)/shard_map/ppermute | solution.py:347
  44.5 0.9 pad_maximum_fusion.2
  45.4 1.6 all-to-all-done
  47.0 3.8 %collective-permute-start.6 = (bf16[300,576]{0,1:T(8,128)(2,1)S(1)}, bf16[300,576]{0,1:T(8,128)(2,1)S(1)}, u32[]{:S(2)}, u32[]{:S(2)}) collective-permute-start(bf16[300,576]{0,1:T(8,128)(2,1)S(1)} %pad_maximum_fusion.4), channel_id=1, source_target_pairs={{0,8},{4,12},{8,0},{12,4},{1,9},{5,13},{9,1},{13,5},{2,10},{6,14},... | collective-permute-start | bytes 1036808 | tf_op jit(solution)/shard_map/ppermute | solution.py:351
  50.8 35.9 %spatial.1 = bf16[512,1152]{1,0:T(8,128)(2,1)} custom-call(bf16[512,1152]{1,0:T(8,128)(2,1)} %bitcast.47, bf16[512,1152]{1,0:T(8,128)(2,1)} %collective-permute-done.4.other, bf16[1152,3456]{1,0:T(8,128)(2,1)} %wqkv.1, bf16[1152,1152]{1,0:T(8,128)(2,1)} %wout.1, f32[6,1152]{1,0:T(8,128)} %mod.3, f32[1,1152]{1,0:T(1,128)} %reshape_tile.9.gain), custom_call_target="tpu_custom_call" | custom-call | flops 30000001024 | bytes 20000000 | tf_op jit(solution)/shard_map/spatial/pallas_call | solution.py:142
  87.5 30.3 %all_to_all.15 = bf16[64,8,1152]{2,1,0:T(8,128)(2,1)} all-to-all(bf16[64,8,1152]{2,1,0:T(8,128)(2,1)} %bitcast.49), channel_id=1, replica_groups=mesh['x'=4,'zh'=2,'y'=4,'zl'=2,'c'=2] {'y','zl','x','zh'}, dimensions={0} | all-to-all | bytes 2359296 | tf_op jit(solution)/shard_map/all_to_all | solution.py:386
  118.7 1.4 pad_maximum_fusion
  120.3 27.5 %temporal.1 = bf16[512,1152]{1,0:T(8,128)(2,1)} custom-call(s32[2]{0:T(128)} %pad_add_fusion.place, bf16[32,2,80,1152]{3,2,1,0:T(8,128)(2,1)} %bitcast.57, bf16[512,1152]{1,0:T(8,128)(2,1)} %bitcast.45, f32[256,1]{1,0:T(8,128)} %copy.16.valid, f32[6,1152]{1,0:T(8,128)} %mod.3, f32[1,1152]{1,0:T(1,128)} %reshape_tile.10.gain), custom_call_target="tpu_custom_call" | custom-call | flops 20000000000 | bytes 20000000 | tf_op jit(solution)/shard_map/temporal/pallas_call | solution.py:242
  147.9 4.3 %all-to-all-start.2 = ((bf16[8,64,1152]{2,1,0:T(8,128)(2,1)}), bf16[8,64,1152]{2,1,0:T(8,128)(2,1)}, u32[]{:S(2)}, u32[]{:S(2)}) async-start(bf16[8,64,1152]{2,1,0:T(8,128)(2,1)} %bitcast.48), calls=%async_computation.2 | async-start | bytes 2359296 | tf_op jit(solution)/shard_map/all_to_all | solution.py:394
  152.5 1.1 fusion
  153.7 1.4 copy.17
  155.6 2.1 %pad_maximum_fusion.3.tk = bf16[304,1152]{1,0:T(8,128)(2,1)} fusion(bf16[4,1152]{1,0:T(4,128)(2,1)S(1)} %reshape.58, bf16[300,1152]{1,0:T(8,128)(2,1)} %copy.17), kind=kLoop, calls=%fused_computation.5 | loop fusion | flops 1400832 | bytes 1400832 | tf_op jit(solution)/shard_map/jit(_pad)/concatenate | solution.py:388
  157.6 1.4 pad_convert_fusion.tvt
  159.0 8.7 %all-to-all-done.2 = bf16[8,64,1152]{2,1,0:T(8,128)(2,1)} async-done(((bf16[8,64,1152]{2,1,0:T(8,128)(2,1)}), bf16[8,64,1152]{2,1,0:T(8,128)(2,1)}, u32[]{:S(2)}, u32[]{:S(2)}) %all-to-all-start.2) | async-done | bytes 1179680 | tf_op jit(solution)/shard_map/all_to_all | solution.py:394
  167.7 17.2 %cross.1 = bf16[8,64,1152]{2,1,0:T(8,128)(2,1)} custom-call(s32[2]{0:T(128)} %pad_add_fusion.place, bf16[8,2,80,2304]{3,2,1,0:T(8,128)(2,1)} %bitcast.58, bf16[512,1152]{1,0:T(8,128)(2,1)} %bitcast.16.x, bf16[304,1152]{1,0:T(8,128)(2,1)} %pad_maximum_fusion.3.tk, f32[1152,304]{1,0:T(8,128)} %pad_convert_fusion.tvt), custom_call_target="tpu_custom_call" | custom-call | flops 20000000000 | bytes 20000000 | tf_op jit(solution)/shard_map/cross/pallas_call | solution.py:300
  (52 shorter events, 6.4 us)
Async XLA Ops:
  6.5 1.1 copy-start
  6.5 113.8 %all-gather.7.cloned.1.call-start = ((), (), s32[]{:S(2)}) async-start(), calls=%async_computation.4 | async-start | bytes 12165120 | tf_op jit(solution)/shard_map/all_gather | solution.py:371
  9.0 1.4 collective-permute-start
  10.4 9.1 %collective-permute-start.1 = (bf16[80,1152]{1,0:T(8,128)(2,1)S(1)}, bf16[80,1152]{1,0:T(8,128)(2,1)S(1)}, u32[]{:S(2)}, u32[]{:S(2)}) collective-permute-start(bf16[80,1152]{1,0:T(8,128)(2,1)S(1)} %dynamic_slice.20), channel_id=1, source_target_pairs={{0,18},{18,0},{2,16},{16,2},{1,19},{19,1},{3,17},{17,3},{4,22},{22... | collective-permute-start | bytes 552968 | tf_op jit(solution)/shard_map/ppermute | solution.py:334
  15.5 9.8 %copy-start.5 = (f32[4,72]{1,0:T(4,128)S(1)}, f32[4,72]{1,0:T(4,128)}, u32[]{:S(2)}) copy-start(f32[4,72]{1,0:T(4,128)} %param.13) | copy-start | bytes 3460
  20.3 6.6 %copy-start.6 = (s32[64]{0:T(128)S(1)}, s32[64]{0:T(128)}, u32[]{:S(2)}) copy-start(s32[64]{0:T(128)} %param.10) | copy-start | bytes 772
  20.3 26.7 %all-to-all-start = ((bf16[8,64,1152]{2,1,0:T(8,128)(2,1)}), bf16[8,64,1152]{2,1,0:T(8,128)(2,1)S(1)}, u32[]{:S(2)}, u32[]{:S(2)}) async-start(bf16[8,64,1152]{2,1,0:T(8,128)(2,1)} %param.9), calls=%async_computation | async-start | bytes 2359296 | tf_op jit(solution)/shard_map/all_to_all | solution.py:364
  25.3 133.7 %all-gather.5.cloned.1.call-start = ((), (), s32[]{:S(2)}) async-start(), calls=%async_computation.3 | async-start | bytes 6635520 | tf_op jit(solution)/shard_map/all_gather | solution.py:391
  25.4 18.9 %collective-permute-start.3 = (bf16[300,288]{0,1:T(8,128)(2,1)S(1)}, bf16[300,288]{0,1:T(8,128)(2,1)S(1)}, u32[]{:S(2)}, u32[]{:S(2)}) collective-permute-start(bf16[300,288]{0,1:T(8,128)(2,1)S(1)} %pad_maximum_fusion.6), channel_id=1, source_target_pairs={{0,2},{2,0},{1,3},{3,1},{4,6},{6,4},{5,7},{7,5},{8,10},{10,8},{9,1... | collective-permute-start | bytes 518408 | tf_op jit(solution)/shard_map/ppermute | solution.py:347
  26.9 17.5 %collective-permute-start.2 = (bf16[80,2304]{1,0:T(8,128)(2,1)S(1)}, bf16[80,2304]{1,0:T(8,128)(2,1)S(1)}, u32[]{:S(2)}, u32[]{:S(2)}) collective-permute-start(bf16[80,2304]{1,0:T(8,128)(2,1)S(1)} %constant_dynamic-slice_fusion.4), channel_id=1, source_target_pairs={{0,18},{18,0},{2,16},{16,2},{1,19},{19,1},{3,17},{17,3},{4,22},{22... | collective-permute-start | bytes 1105928 | tf_op jit(solution)/shard_map/ppermute | solution.py:334
  47.0 3.8 %copy-start.2 = (bf16[8,64,1152]{2,1,0:T(8,128)(2,1)}, bf16[8,64,1152]{2,1,0:T(8,128)(2,1)S(1)}, u32[]{:S(2)}) copy-start(bf16[8,64,1152]{2,1,0:T(8,128)(2,1)S(1)} %all-to-all-done) | copy-start | bytes 3538948
  47.0 3.8 %collective-permute-start.4 = (bf16[512,1152]{1,0:T(8,128)(2,1)S(1)}, bf16[512,1152]{1,0:T(8,128)(2,1)}, u32[]{:S(2)}, u32[]{:S(2)}) collective-permute-start(bf16[512,1152]{1,0:T(8,128)(2,1)S(1)} %bitcast.46), channel_id=1, source_target_pairs={{0,1},{1,0},{2,3},{3,2},{4,5},{5,4},{6,7},{7,6},{8,9},{9,8},{10,11... | collective-permute-start | bytes 3538952 | tf_op jit(solution)/shard_map/ppermute | solution.py:338
  47.0 39.7 %collective-permute-start.5 = (bf16[300,576]{0,1:T(8,128)(2,1)S(1)}, bf16[300,576]{0,1:T(8,128)(2,1)S(1)}, u32[]{:S(2)}, u32[]{:S(2)}) collective-permute-start(bf16[300,576]{0,1:T(8,128)(2,1)S(1)} %pad_maximum_fusion.4), channel_id=1, source_target_pairs={{0,4},{4,8},{8,12},{12,0},{1,5},{5,9},{9,13},{13,1},{2,6},{6,10},{... | collective-permute-start | bytes 1036808 | tf_op jit(solution)/shard_map/ppermute | solution.py:351
  47.0 39.7 %collective-permute-start.6 = (bf16[300,576]{0,1:T(8,128)(2,1)S(1)}, bf16[300,576]{0,1:T(8,128)(2,1)S(1)}, u32[]{:S(2)}, u32[]{:S(2)}) collective-permute-start(bf16[300,576]{0,1:T(8,128)(2,1)S(1)} %pad_maximum_fusion.4), channel_id=1, source_target_pairs={{0,8},{4,12},{8,0},{12,4},{1,9},{5,13},{9,1},{13,5},{2,10},{6,14},... | collective-permute-start | bytes 1036808 | tf_op jit(solution)/shard_map/ppermute | solution.py:351
  50.8 35.9 %collective-permute-start.7 = (bf16[300,576]{0,1:T(8,128)(2,1)S(1)}, bf16[300,576]{0,1:T(8,128)(2,1)}, u32[]{:S(2)}, u32[]{:S(2)}) collective-permute-start(bf16[300,576]{0,1:T(8,128)(2,1)S(1)} %pad_maximum_fusion.4), channel_id=1, source_target_pairs={{0,12},{4,0},{8,4},{12,8},{1,13},{5,1},{9,5},{13,9},{2,14},{6,2},{... | collective-permute-start | bytes 1036808 | tf_op jit(solution)/shard_map/ppermute | solution.py:351
  86.7 0.8 copy-start.3
  87.5 31.2 %copy-start.4 = (bf16[300,576]{0,1:T(8,128)(2,1)S(1)}, bf16[300,576]{0,1:T(8,128)(2,1)}, u32[]{:S(2)}) copy-start(bf16[300,576]{0,1:T(8,128)(2,1)} %copy-done.3) | copy-start | bytes 1036804
  147.9 19.9 %all-to-all-start.2 = ((bf16[8,64,1152]{2,1,0:T(8,128)(2,1)}), bf16[8,64,1152]{2,1,0:T(8,128)(2,1)}, u32[]{:S(2)}, u32[]{:S(2)}) async-start(bf16[8,64,1152]{2,1,0:T(8,128)(2,1)} %bitcast.48), calls=%async_computation.2 | async-start | bytes 2359296 | tf_op jit(solution)/shard_map/all_to_all | solution.py:394
  155.1 2.5 %copy-start.1 = (bf16[300,16,1,72]{0,3,2,1:T(8,128)(2,1)S(1)}, bf16[300,16,1,72]{0,3,2,1:T(8,128)(2,1)}, u32[]{:S(2)}) copy-start(bf16[300,16,1,72]{0,3,2,1:T(8,128)(2,1)} %get-tuple-element.39) | copy-start | bytes 2073604
Sparse Core Ops, SparseCore 0:
  20.4 75.9 all-gather.6
  118.0 36.0 all-gather.4
where the time goes:
time: 194 us; the launch traced here: 192 us
  Pallas kernels  80.6 us (42%)
  blocking collectives  30.3 us (16%)
  waiting for transfers between devices  26.9 us (14%)
  starting transfers between devices  21.6 us (11%)
  between operations  13.6 us (7%)
  local copies, waits for them, and re-layouts  9.17 us (5%)
  other arithmetic  8.17 us (4%)
    pallas_call x1, Pallas kernels, spatial(): pl.pallas_call(functools.partial(spatial_kernel, rows=rows), out_shape=ja...  35.9 us
    all_to_all x1, blocking collectives, per_device(): lax.all_to_all(after_spatial.reshape(64, 8, D), YZ + XZ, 0, 0, tiled=True)  30.3 us
    pallas_call x1, Pallas kernels, temporal(): pl.pallas_call(functools.partial(temporal_kernel, rows=rows, frames=64),...  27.5 us
    pallas_call x1, Pallas kernels, cross(): pl.pallas_call(cross_kernel, out_shape=jax.ShapeDtypeStruct((8, rows // 8...  17.2 us
    ppermute x1, waiting for transfers between devices, pos_quad(): return both(pair, 'zl', lax.ppermute(pair, 'zl', SWAP))  12.1 us
    all_to_all x1, waiting for transfers between devices, per_device(): lax.all_to_all(after_temporal.reshape(8, 64, D), XZ, 0, 0, tiled=True)  8.73 us
    ppermute x2, starting transfers between devices, across(): return lax.ppermute(v, ('zh', 'zl'), ACROSS)  6.96 us
    all_to_all x1, starting transfers between devices, per_device(): own = lax.all_to_all(tokens, YZ, 0, 0, tiled=True).reshape(-1, D)  4.96 us
  transfers between devices with their start and end apart: 12, of which 5 were waited for; matrix products, arithmetic and copies ran while one was open for 8% of the time, Pallas kernels for 33%

commit v1 on v0

--- a/solution.py
+++ b/solution.py
@@ -99,21 +99,39 @@
         run(True)
 
 
-def spatial_kernel(own, other, wqkv, wout, mod, gain, out, xin, k, qt, vt, at, *, rows):
+def spatial_kernel(own_hbm, other_hbm, wqkv_hbm, wout_hbm, mod, gain, out, own, other, wqkv, wout, xin, k, qt, vt, at, sems, *, rows):
+    copies = [pltpu.make_async_copy(own_hbm, own, sems.at[0]), pltpu.make_async_copy(other_hbm, other, sems.at[1])]
+    for i in range(3):
+        columns = pl.ds(D * i, D)
+        copies.append(pltpu.make_async_copy(wqkv_hbm.at[:, columns], wqkv.at[:, columns], sems.at[2 + i]))
+    copies.append(pltpu.make_async_copy(wout_hbm, wout, sems.at[5]))
+    for copy in copies:
+        copy.start()
     gather, spread = indicators()
     shift, scale, gate = mod[0:1, :], mod[1:2, :], mod[2:3, :]
     R = 256
-    for b in range(rows // R):
-        sl = pl.ds(b * R, R)
+
+    def block(i):
+        return pl.ds(pl.multiple_of(i * R, R), R)
+
+    def normed(i):
+        sl, far = block(i), block(i + rows // R)
         xin[sl, :] = norm_rows(own[sl, :].astype(F32), shift, scale)
-        xin[pl.ds(rows + b * R, R), :] = norm_rows(other[sl, :].astype(F32), shift, scale)
-    for b in range(rows // R):
-        sl = pl.ds(b * R, R)
+        xin[far, :] = norm_rows(other[sl, :].astype(F32), shift, scale)
+
+    def project(i):
+        sl, far = block(i), block(i + rows // R)
         qt[:, sl] = dot(xin[sl, :], wqkv[:, 0:D]).T
-    for b in range(2 * rows // R):
-        sl = pl.ds(b * R, R)
-        k[sl, :] = head_norm_rows(dot(xin[sl, :], wqkv[:, D:2 * D]), gather, spread, gain[...])
-        vt[:, sl] = dot(xin[sl, :], wqkv[:, 2 * D:]).T
+        for to in (sl, far):
+            k[to, :] = head_norm_rows(dot(xin[to, :], wqkv[:, D:2 * D]), gather, spread, gain[...])
+            vt[:, to] = dot(xin[to, :], wqkv[:, 2 * D:]).T
+
+    for copy in copies[:2]:
+        copy.wait()
+    loop(rows // R, normed)
+    for copy in copies[2:5]:
+        copy.wait()
+    loop(rows // R, project)
 
     def run(shifted):
         def pair(i):
@@ -127,13 +145,18 @@
         loop(HEADS // 2, pair)
 
     guarded(gain, run)
-    for b in range(rows // R):
-        sl = pl.ds(b * R, R)
+
+    def finish(i):
+        sl = block(i)
         proj = dot(at[:, sl].T.astype(BF), wout[...])
         out[sl, :] = (own[sl, :].astype(F32) + gate * proj).astype(BF)
 
+    copies[5].wait()
+    loop(rows // R, finish)
+
 
 VMEM = pl.BlockSpec(memory_space=pltpu.VMEM)
+HBM = pl.BlockSpec(memory_space=pl.ANY)
 PARAMS = pltpu.CompilerParams(vmem_limit_bytes=60 * 2**20)
 
 
@@ -142,14 +165,19 @@
     return pl.pallas_call(
         functools.partial(spatial_kernel, rows=rows),
         out_shape=jax.ShapeDtypeStruct((rows, D), BF),
-        in_specs=[VMEM] * 6,
+        in_specs=[HBM] * 4 + [VMEM] * 2,
         out_specs=VMEM,
         scratch_shapes=[
+            pltpu.VMEM((rows, D), BF),
+            pltpu.VMEM((rows, D), BF),
+            pltpu.VMEM((D, 3 * D), BF),
+            pltpu.VMEM((D, D), BF),
             pltpu.VMEM((2 * rows, D), BF),
             pltpu.VMEM((2 * rows, D), BF),
             pltpu.VMEM((D, rows), F32),
             pltpu.VMEM((D, 2 * rows), F32),
             pltpu.VMEM((D, rows), F32),
+            pltpu.SemaphoreType.DMA((6,)),
         ],
         compiler_params=PARAMS,
         cost_estimate=pl.CostEstimate(flops=3 * 10**10, bytes_accessed=2 * 10**7, transcendentals=0),
@@ -162,8 +190,8 @@
     width = gathered.shape[3]
     parts = weight.shape[1] // width
     copies = []
-    for x in range(4):
-        for y in range(parts):
+    for y in range(parts):
+        for x in range(4):
             for core in range(2):
                 low, count = (0, HALF) if core == 0 else (HALF - 64, 64)
                 for dz in range(2):
@@ -181,7 +209,7 @@
     return (source == source_of(to)).astype(F32).astype(BF)
 
 
-def temporal_kernel(place, gathered, x, valid, mod, gain, out, w, xp, xin, k, qt, vt, at, sems, *, rows, frames):
+def temporal_kernel(place, gathered, x, mod, gain, out, w, xp, xin, k, qt, vt, at, sems, *, rows, frames):
     copies = piece_copies(place, gathered, w, sems)
     for copy in copies:
         copy.start()
@@ -195,7 +223,7 @@
         moved = dot(order[b * R:(b + 1) * R, :], x[...])
         xp[sl, :] = moved.astype(BF)
         xin[sl, :] = norm_rows(moved, shift, scale)
-    for copy in copies:
+    for copy in copies[:48]:
         copy.wait()
     for b in range(rows // R):
         sl = pl.ds(b * R, R)
@@ -203,9 +231,11 @@
         k[sl, :] = head_norm_rows(dot(xin[sl, :], w[:, D:2 * D]), gather, spread, gain[...])
         vt[:, sl] = dot(xin[sl, :], w[:, 2 * D:3 * D]).T
 
-    key = lax.broadcasted_iota(jnp.int32, (R, R), 0) // frames
+    row = lax.broadcasted_iota(jnp.int32, (R, R), 0)
+    held = lax.rem(row, frames)
+    frame = lax.rem(held, frames // 8) * 8 + held // (frames // 8)
     query = lax.broadcasted_iota(jnp.int32, (R, R), 1) // frames
-    bias = jnp.where(key == query, 0.0, -1e30) + valid[...]
+    bias = jnp.where((row // frames == query) & (frame < place[2]), 0.0, -1e30)
 
     def run(shifted):
         def pair(i):
@@ -221,6 +251,8 @@
         loop(HEADS // 2, pair)
 
     guarded(gain, run)
+    for copy in copies[48:]:
+        copy.wait()
     for b in range(rows // R):
         sl = pl.ds(b * R, R)
         proj = dot(at[:, sl].T.astype(BF), w[:, 3 * D:])
@@ -236,13 +268,12 @@
         out[pl.ds(b * R, R), :] = dot(order[b * R:(b + 1) * R, :], xin[...]).astype(BF)
 
 
-def temporal(place, gathered, x, valid, mod, gain):
+def temporal(place, gathered, x, mod, gain):
     rows = x.shape[0]
-    hbm = pl.BlockSpec(memory_space=pl.ANY)
     return pl.pallas_call(
         functools.partial(temporal_kernel, rows=rows, frames=64),
         out_shape=jax.ShapeDtypeStruct((rows, D), BF),
-        in_specs=[pl.BlockSpec(memory_space=pltpu.SMEM)] + [hbm] + [VMEM] * 4,
+        in_specs=[pl.BlockSpec(memory_space=pltpu.SMEM)] + [HBM] + [VMEM] * 3,
         out_specs=VMEM,
         scratch_shapes=[
             pltpu.VMEM((D, 4 * D), BF),
@@ -257,7 +288,7 @@
         compiler_params=PARAMS,
         cost_estimate=pl.CostEstimate(flops=2 * 10**10, bytes_accessed=2 * 10**7, transcendentals=0),
         name="temporal",
-    )(place, gathered, x, valid, mod, gain)
+    )(place, gathered, x, mod, gain)
 
 
 def cross_kernel(place, gathered, x, tk, tvt, out, w, qt, at, sems):
@@ -296,11 +327,10 @@
 
 def cross(place, gathered, x, tk, tvt):
     rows = x.shape[0]
-    hbm = pl.BlockSpec(memory_space=pl.ANY)
     return pl.pallas_call(
         cross_kernel,
         out_shape=jax.ShapeDtypeStruct((8, rows // 8, D), BF),
-        in_specs=[pl.BlockSpec(memory_space=pltpu.SMEM)] + [hbm] + [VMEM] * 3,
+        in_specs=[pl.BlockSpec(memory_space=pltpu.SMEM)] + [HBM] + [VMEM] * 3,
         out_specs=VMEM,
         scratch_shapes=[
             pltpu.VMEM((D, 2 * D), BF),
@@ -338,13 +368,9 @@
     return lax.ppermute(v, "c", SWAP)
 
 
-def pos_quad(local, swapped):
-    def both(v, axis, other):
-        first = lax.axis_index(axis) == 0
-        return jnp.concatenate([jnp.where(first, v, other), jnp.where(first, other, v)], 1)
-
-    pair = both(local, "c", swapped)
-    return both(pair, "zl", lax.ppermute(pair, "zl", SWAP))
+def in_pairs(v, axis, other):
+    first = lax.axis_index(axis) == 0
+    return jnp.concatenate([jnp.where(first, v, other), jnp.where(first, other, v)], 1)
 
 
 def along_y(quad):
@@ -359,38 +385,38 @@
 
 def per_device(tokens, frame_valid, text, modulation, qk_gains, spatial_qkv, spatial_out, block_weights, cross_kv):
     core, y = lax.axis_index("c"), lax.axis_index("y")
-    local = jnp.dot(text, cross_kv.reshape(D, 2 * HD), preferred_element_type=F32).astype(BF)
-    swapped = swap(local)
     own = lax.all_to_all(tokens, YZ, 0, 0, tiled=True).reshape(-1, D)
     w1 = lax.dynamic_slice(block_weights, (64 * core, D * y), (HALF, D))
-    w1, swapped = bar((w1, swapped))
-    z1 = across(w1)
-    both1 = jnp.stack([w1, z1])
     w2 = lax.dynamic_slice(block_weights, (64 * core, 4 * D), (HALF, 2 * D))
-    w2, both1 = bar((w2, both1))
-    gathered1 = lax.all_gather(both1, ("x", "y", "c"), axis=0)
-    both2 = jnp.stack([w2, across(w2)])
-    quad = pos_quad(local, swapped)
+    both1 = jnp.stack([w1, across(w1)])
+    local = jnp.dot(text, cross_kv.reshape(D, 2 * HD), preferred_element_type=F32).astype(BF)
     gain_s = gains(qk_gains[0], qk_gains[1])
     gain_t = gains(qk_gains[2], qk_gains[3])
-    seen = jnp.where(frame_valid.reshape(8, 8).T.reshape(64) > 0, 0.0, -1e30)
-    valid = jnp.tile(seen, 4).reshape(256, 1).astype(F32)
-    place = jnp.stack([lax.axis_index("zh"), core]).astype(jnp.int32)
-    own, both2, quad, gain_s, gain_t, valid, place = bar((own, both2, quad, gain_s, gain_t, valid, place))
+    count = jnp.sum((frame_valid > 0).astype(jnp.int32))
+    place = jnp.stack([lax.axis_index("zh"), core, count]).astype(jnp.int32)
+    both1, local, gain_s, gain_t, place = bar((both1, local, gain_s, gain_t, place))
+    gathered1 = lax.all_gather(both1, ("x", "y", "c"), axis=0)
+    own, local, w2 = bar((own, local, w2))
 
     other = swap(own)
-    steps = along_y(quad)
+    swapped = swap(local)
+    z2 = across(w2)
     after_spatial = spatial(own, other, spatial_qkv, spatial_out, modulation, gain_s)
-    after_spatial, steps = bar((after_spatial, steps))
+    after_spatial, swapped, z2 = bar((after_spatial, swapped, z2))
 
     rows = lax.all_to_all(after_spatial.reshape(64, 8, D), YZ + XZ, 0, 0, tiled=True).reshape(-1, D)
+    pair = in_pairs(local, "c", swapped)
+    besides = lax.ppermute(pair, "zl", SWAP)
+    rows, besides = bar((rows, besides))
+    steps = along_y(in_pairs(pair, "zl", besides))
+    _, both2 = bar((rows, jnp.stack([w2, z2])))
+    gathered2 = lax.all_gather(both2, ("x", "c"), axis=0)
+    after_temporal = temporal(place, gathered1, rows, modulation, gain_t)
+    after_temporal, steps = bar((after_temporal, steps))
+
     every = in_order(steps).reshape(TEXT, HEADS, 2, HD)
     tk = jnp.pad(every[:, :, 0].reshape(TEXT, D), ((0, TPAD - TEXT), (0, 0)), mode="edge")
     tvt = jnp.pad(every[:, :, 1].reshape(TEXT, D).T, ((0, 0), (0, TPAD - TEXT))).astype(F32)
-    _, both2 = bar((rows, both2))
-    gathered2 = lax.all_gather(both2, ("x", "c"), axis=0)
-    after_temporal = temporal(place, gathered1, rows, valid, modulation, gain_t)
-
     back = lax.all_to_all(after_temporal.reshape(8, 64, D), XZ, 0, 0, tiled=True).reshape(-1, D)
     return cross(place, gathered2, back, tk, tvt)
 

time: 194 us -> 191 us (0.985)
  blocking collectives: 30.3 us -> 0 us
  waiting for transfers between devices: 26.9 us -> 50.9 us
  starting transfers between devices: 21.6 us -> 29.4 us
  local copies, waits for them, and re-layouts: 9.17 us -> 5.65 us
    all_to_all x1 -> x0, blocking collectives: 30.3 us -> none  [per_device(): lax.all_to_all(after_spatial.reshape(64, 8, D), YZ + XZ, 0, 0, tiled=True)]
    all_to_all x1, waiting for transfers between devices: 1.63 us -> 20.5 us  [per_device(): own = lax.all_to_all(tokens, YZ, 0, 0, tiled=True).reshape(-1, D)]
    all_to_all x0 -> x1, starting transfers between devices: none -> 7.42 us  [per_device(): lax.all_to_all(after_spatial.reshape(64, 8, D), YZ + XZ, 0, 0, tiled=True)]
    ppermute x1, waiting for transfers between devices: 12.1 us -> 16.6 us  [per_device(): besides = lax.ppermute(pair, 'zl', SWAP)]
    ppermute x2, waiting for transfers between devices: 4 us -> 0.01 us  [across(): return lax.ppermute(v, ('zh', 'zl'), ACROSS)]
    ppermute x2, starting transfers between devices: 6.96 us -> 4.12 us  [across(): return lax.ppermute(v, ('zh', 'zl'), ACROSS)]
    ppermute x1, starting transfers between devices: 3.8 us -> 1.1 us  [along_y(): lax.ppermute(quad, 'y', [(i, (i + 2) % 4) for i in range(4)])]
    ppermute x2, waiting for transfers between devices: 0.35 us -> 2.63 us  [swap(): return lax.ppermute(v, 'c', SWAP)]
  transfers between devices with their start and end apart: 12 -> 13, of which waited for: 5 -> 5; matrix products, arithmetic and copies ran while one was open for 8% -> 8% of each run, Pallas kernels for 33% -> 33%
where the time goes in v1:
time: 191 us; the launch traced here: 190 us
  Pallas kernels  79.1 us (41%)
  waiting for transfers between devices  50.9 us (27%)
  starting transfers between devices  29.4 us (15%)
  between operations  13.6 us (7%)
  other arithmetic  9.8 us (5%)
  local copies, waits for them, and re-layouts  5.65 us (3%)
    pallas_call x1, Pallas kernels, spatial(): pl.pallas_call(functools.partial(spatial_kernel, rows=rows), out_shape=ja...  35.9 us
    pallas_call x1, Pallas kernels, temporal(): pl.pallas_call(functools.partial(temporal_kernel, rows=rows, frames=64),...  26.1 us
    all_to_all x1, waiting for transfers between devices, per_device(): own = lax.all_to_all(tokens, YZ, 0, 0, tiled=True).reshape(-1, D)  20.5 us
    pallas_call x1, Pallas kernels, cross(): pl.pallas_call(cross_kernel, out_shape=jax.ShapeDtypeStruct((8, rows // 8...  17.2 us
    ppermute x1, waiting for transfers between devices, per_device(): besides = lax.ppermute(pair, 'zl', SWAP)  16.6 us
    all_to_all x1, waiting for transfers between devices, per_device(): lax.all_to_all(after_temporal.reshape(8, 64, D), XZ, 0, 0, tiled=True)  10.8 us
    all_to_all x1, starting transfers between devices, per_device(): lax.all_to_all(after_spatial.reshape(64, 8, D), YZ + XZ, 0, 0, tiled=True)  7.42 us
    all_to_all x1, starting transfers between devices, per_device(): lax.all_to_all(after_temporal.reshape(8, 64, D), XZ, 0, 0, tiled=True)  6.32 us
  transfers between devices with their start and end apart: 13, of which 5 were waited for; matrix products, arithmetic and copies ran while one was open for 8% of the time, Pallas kernels for 33%

profile of v1, /device:TPU:8, one launch (start us, length us, event | category | flops | bytes accessed | tf_op | source)
XLA Modules:
  0.0 190.0 jit_solution(8610474313386818601)
XLA Ops:
  6.5 1.0 dynamic_slice.19
  7.5 4.1 %collective-permute-start = (bf16[80,1152]{1,0:T(8,128)(2,1)S(1)}, bf16[80,1152]{1,0:T(8,128)(2,1)S(1)}, u32[]{:S(2)}, u32[]{:S(2)}) collective-permute-start(bf16[80,1152]{1,0:T(8,128)(2,1)S(1)} %dynamic_slice.19), channel_id=1, source_target_pairs={{0,18},{18,0},{2,16},{16,2},{1,19},{19,1},{3,17},{17,3},{4,22},{22... | collective-permute-start | bytes 552968 | tf_op jit(solution)/shard_map/ppermute | solution.py:364
  11.7 1.3 fusion
  15.2 1.4 convolution_convert_fusion
  16.6 1.3 pad_add_fusion.place
  17.9 0.9 dynamic-slice_bitcast_fusion
  19.7 5.0 %all-to-all-start = ((bf16[8,64,1152]{2,1,0:T(8,128)(2,1)}), bf16[8,64,1152]{2,1,0:T(8,128)(2,1)S(1)}, u32[]{:S(2)}, u32[]{:S(2)}) async-start(bf16[8,64,1152]{2,1,0:T(8,128)(2,1)} %param.9), calls=%async_computation | async-start | bytes 2359296 | tf_op jit(solution)/shard_map/all_to_all | solution.py:388
  24.6 1.0 constant_dynamic-slice_fusion.4
  25.6 20.5 %all-to-all-done = bf16[8,64,1152]{2,1,0:T(8,128)(2,1)S(1)} async-done(((bf16[8,64,1152]{2,1,0:T(8,128)(2,1)}), bf16[8,64,1152]{2,1,0:T(8,128)(2,1)S(1)}, u32[]{:S(2)}, u32[]{:S(2)}) %all-to-all-start) | async-done | bytes 1179680 | tf_op jit(solution)/shard_map/all_to_all | solution.py:388
  46.7 2.6 %collective-permute-done.1.other_hbm = bf16[512,1152]{1,0:T(8,128)(2,1)} collective-permute-done((bf16[512,1152]{1,0:T(8,128)(2,1)S(1)}, bf16[512,1152]{1,0:T(8,128)(2,1)}, u32[]{:S(2)}, u32[]{:S(2)}) %collective-permute-start.1) | collective-permute-done | bytes 1179680 | tf_op jit(solution)/shard_map/ppermute | solution.py:368
  49.3 35.9 %spatial.1 = bf16[512,1152]{1,0:T(8,128)(2,1)} custom-call(bf16[512,1152]{1,0:T(8,128)(2,1)} %bitcast.50, bf16[512,1152]{1,0:T(8,128)(2,1)} %collective-permute-done.1.other_hbm, bf16[1152,3456]{1,0:T(8,128)(2,1)} %wqkv_hbm.1, bf16[1152,1152]{1,0:T(8,128)(2,1)} %wout_hbm.1, f32[6,1152]{1,0:T(8,128)} %mod.3, f32[1,1152]{1,0:T(1,128)} %reshape_tile.6.gain), custom_call_target="tpu_custom_call" | custom-call | flops 30000001024 | bytes 20000000 | tf_op jit(solution)/shard_map/spatial/pallas_call | solution.py:165
  85.2 7.4 %all-to-all-start.1 = ((bf16[64,8,1152]{2,1,0:T(8,128)(2,1)}), bf16[64,8,1152]{2,1,0:T(8,128)(2,1)S(1)}, u32[]{:S(2)}, u32[]{:S(2)}) async-start(bf16[64,8,1152]{2,1,0:T(8,128)(2,1)} %bitcast.48), calls=%async_computation.1 | async-start | bytes 2359296 | tf_op jit(solution)/shard_map/all_to_all | solution.py:407
  92.7 1.6 collective-permute-start.4
  94.3 0.9 pad_maximum_fusion.2
  95.3 16.6 %collective-permute-done.4 = bf16[300,288]{0,1:T(8,128)(2,1)S(1)} collective-permute-done((bf16[300,288]{0,1:T(8,128)(2,1)S(1)}, bf16[300,288]{0,1:T(8,128)(2,1)S(1)}, u32[]{:S(2)}, u32[]{:S(2)}) %collective-permute-start.4) | collective-permute-done | bytes 172832 | tf_op jit(solution)/shard_map/ppermute | solution.py:409
  112.4 1.4 collective-permute-start.7
  113.8 1.1 collective-permute-start.6
  114.9 2.0 %collective-permute-start.5 = (bf16[300,576]{0,1:T(8,128)(2,1)S(1)}, bf16[300,576]{0,1:T(8,128)(2,1)}, u32[]{:S(2)}, u32[]{:S(2)}) collective-permute-start(bf16[300,576]{0,1:T(8,128)(2,1)S(1)} %pad_maximum_fusion.4), channel_id=1, source_target_pairs={{0,4},{4,8},{8,12},{12,0},{1,5},{5,9},{9,13},{13,1},{2,6},{6,10},{... | collective-permute-start | bytes 1036808 | tf_op jit(solution)/shard_map/ppermute | solution.py:377
  116.9 26.1 %temporal.1 = bf16[512,1152]{1,0:T(8,128)(2,1)} custom-call(s32[3]{0:T(128)} %pad_add_fusion.place, bf16[32,2,80,1152]{3,2,1,0:T(8,128)(2,1)} %bitcast.56, bf16[512,1152]{1,0:T(8,128)(2,1)} %bitcast.46, f32[6,1152]{1,0:T(8,128)} %mod.3, f32[1,1152]{1,0:T(1,128)} %reshape_tile.7.gain), custom_call_target="tpu_custom_call" | custom-call | flops 20000000000 | bytes 20000000 | tf_op jit(solution)/shard_map/temporal/pallas_call | solution.py:273
  143.0 6.3 %all-to-all-start.2 = ((bf16[8,64,1152]{2,1,0:T(8,128)(2,1)}), bf16[8,64,1152]{2,1,0:T(8,128)(2,1)}, u32[]{:S(2)}, u32[]{:S(2)}) async-start(bf16[8,64,1152]{2,1,0:T(8,128)(2,1)} %bitcast.47), calls=%async_computation.2 | async-start | bytes 2359296 | tf_op jit(solution)/shard_map/all_to_all | solution.py:420
  149.4 1.4 pad_maximum_fusion
  153.8 1.4 pad_convert_fusion.tvt
  155.1 10.8 %all-to-all-done.2 = bf16[8,64,1152]{2,1,0:T(8,128)(2,1)} async-done(((bf16[8,64,1152]{2,1,0:T(8,128)(2,1)}), bf16[8,64,1152]{2,1,0:T(8,128)(2,1)}, u32[]{:S(2)}, u32[]{:S(2)}) %all-to-all-start.2) | async-done | bytes 1179680 | tf_op jit(solution)/shard_map/all_to_all | solution.py:420
  165.9 17.2 %cross.1 = bf16[8,64,1152]{2,1,0:T(8,128)(2,1)} custom-call(s32[3]{0:T(128)} %pad_add_fusion.place, bf16[8,2,80,2304]{3,2,1,0:T(8,128)(2,1)} %bitcast.57, bf16[512,1152]{1,0:T(8,128)(2,1)} %bitcast.16.x, bf16[304,1152]{1,0:T(8,128)(2,1)} %pad_maximum_fusion.3.tk, f32[1152,304]{1,0:T(8,128)} %pad_convert_fusion.tvt), custom_call_target="tpu_custom_call" | custom-call | flops 20000000000 | bytes 20000000 | tf_op jit(solution)/shard_map/cross/pallas_call | solution.py:330
  (40 shorter events, 7.1 us)
Async XLA Ops:
  6.5 8.6 %copy-start = (bf16[300,1152]{1,0:T(8,128)(2,1)S(1)}, bf16[300,1152]{1,0:T(8,128)(2,1)}, u32[]{:S(2)}) copy-start(bf16[300,1152]{1,0:T(8,128)(2,1)} %param.11) | copy-start | bytes 2073604
  6.5 110.4 %all-gather.7.cloned.1.call-start = ((), (), s32[]{:S(2)}) async-start(), calls=%async_computation.4 | async-start | bytes 12165120 | tf_op jit(solution)/shard_map/all_gather | solution.py:398
  7.5 11.3 %collective-permute-start = (bf16[80,1152]{1,0:T(8,128)(2,1)S(1)}, bf16[80,1152]{1,0:T(8,128)(2,1)S(1)}, u32[]{:S(2)}, u32[]{:S(2)}) collective-permute-start(bf16[80,1152]{1,0:T(8,128)(2,1)S(1)} %dynamic_slice.19), channel_id=1, source_target_pairs={{0,18},{18,0},{2,16},{16,2},{1,19},{19,1},{3,17},{17,3},{4,22},{22... | collective-permute-start | bytes 552968 | tf_op jit(solution)/shard_map/ppermute | solution.py:364
  19.7 26.5 %all-to-all-start = ((bf16[8,64,1152]{2,1,0:T(8,128)(2,1)}), bf16[8,64,1152]{2,1,0:T(8,128)(2,1)S(1)}, u32[]{:S(2)}, u32[]{:S(2)}) async-start(bf16[8,64,1152]{2,1,0:T(8,128)(2,1)} %param.9), calls=%async_computation | async-start | bytes 2359296 | tf_op jit(solution)/shard_map/all_to_all | solution.py:388
  46.2 3.1 %copy-start.2 = (bf16[8,64,1152]{2,1,0:T(8,128)(2,1)}, bf16[8,64,1152]{2,1,0:T(8,128)(2,1)S(1)}, u32[]{:S(2)}) copy-start(bf16[8,64,1152]{2,1,0:T(8,128)(2,1)S(1)} %all-to-all-done) | copy-start | bytes 3538948
  46.2 3.1 %collective-permute-start.1 = (bf16[512,1152]{1,0:T(8,128)(2,1)S(1)}, bf16[512,1152]{1,0:T(8,128)(2,1)}, u32[]{:S(2)}, u32[]{:S(2)}) collective-permute-start(bf16[512,1152]{1,0:T(8,128)(2,1)S(1)} %bitcast.49), channel_id=1, source_target_pairs={{0,1},{1,0},{2,3},{3,2},{4,5},{5,4},{6,7},{7,6},{8,9},{9,8},{10,11... | collective-permute-start | bytes 3538952 | tf_op jit(solution)/shard_map/ppermute | solution.py:368
  46.2 39.0 %collective-permute-start.2 = (bf16[300,144]{0,1:T(8,128)(2,1)S(1)}, bf16[300,144]{0,1:T(8,128)(2,1)S(1)}, u32[]{:S(2)}, u32[]{:S(2)}) collective-permute-start(bf16[300,144]{0,1:T(8,128)(2,1)S(1)} %convolution_convert_fusion), channel_id=1, source_target_pairs={{0,1},{1,0},{2,3},{3,2},{4,5},{5,4},{6,7},{7,6},{8,9},{9,8},{10,11... | collective-permute-start | bytes 259208 | tf_op jit(solution)/shard_map/ppermute | solution.py:368
  46.7 38.5 %collective-permute-start.3 = (bf16[80,2304]{1,0:T(8,128)(2,1)S(1)}, bf16[80,2304]{1,0:T(8,128)(2,1)S(1)}, u32[]{:S(2)}, u32[]{:S(2)}) collective-permute-start(bf16[80,2304]{1,0:T(8,128)(2,1)S(1)} %constant_dynamic-slice_fusion.4), channel_id=1, source_target_pairs={{0,18},{18,0},{2,16},{16,2},{1,19},{19,1},{3,17},{17,3},{4,22},{22... | collective-permute-start | bytes 1105928 | tf_op jit(solution)/shard_map/ppermute | solution.py:364
  85.2 27.0 %all-to-all-start.1 = ((bf16[64,8,1152]{2,1,0:T(8,128)(2,1)}), bf16[64,8,1152]{2,1,0:T(8,128)(2,1)S(1)}, u32[]{:S(2)}, u32[]{:S(2)}) async-start(bf16[64,8,1152]{2,1,0:T(8,128)(2,1)} %bitcast.48), calls=%async_computation.1 | async-start | bytes 2359296 | tf_op jit(solution)/shard_map/all_to_all | solution.py:407
  92.6 62.5 %all-gather.5.cloned.1.call-start = ((), (), s32[]{:S(2)}) async-start(), calls=%async_computation.3 | async-start | bytes 6635520 | tf_op jit(solution)/shard_map/all_gather | solution.py:413
  92.7 19.2 %collective-permute-start.4 = (bf16[300,288]{0,1:T(8,128)(2,1)S(1)}, bf16[300,288]{0,1:T(8,128)(2,1)S(1)}, u32[]{:S(2)}, u32[]{:S(2)}) collective-permute-start(bf16[300,288]{0,1:T(8,128)(2,1)S(1)} %pad_maximum_fusion.6), channel_id=1, source_target_pairs={{0,2},{2,0},{1,3},{3,1},{4,6},{6,4},{5,7},{7,5},{8,10},{10,8},{9,1... | collective-permute-start | bytes 518408 | tf_op jit(solution)/shard_map/ppermute | solution.py:409
  112.2 4.7 %copy-start.1 = (bf16[64,8,1152]{2,1,0:T(8,128)(2,1)}, bf16[64,8,1152]{2,1,0:T(8,128)(2,1)S(1)}, u32[]{:S(2)}) copy-start(bf16[64,8,1152]{2,1,0:T(8,128)(2,1)S(1)} %all-to-all-done.1) | copy-start | bytes 3538948
  112.4 30.6 %collective-permute-start.7 = (bf16[300,576]{0,1:T(8,128)(2,1)S(1)}, bf16[300,576]{0,1:T(8,128)(2,1)S(1)}, u32[]{:S(2)}, u32[]{:S(2)}) collective-permute-start(bf16[300,576]{0,1:T(8,128)(2,1)S(1)} %pad_maximum_fusion.4), channel_id=1, source_target_pairs={{0,12},{4,0},{8,4},{12,8},{1,13},{5,1},{9,5},{13,9},{2,14},{6,2},{... | collective-permute-start | bytes 1036808 | tf_op jit(solution)/shard_map/ppermute | solution.py:377
  113.8 29.2 %collective-permute-start.6 = (bf16[300,576]{0,1:T(8,128)(2,1)S(1)}, bf16[300,576]{0,1:T(8,128)(2,1)S(1)}, u32[]{:S(2)}, u32[]{:S(2)}) collective-permute-start(bf16[300,576]{0,1:T(8,128)(2,1)S(1)} %pad_maximum_fusion.4), channel_id=1, source_target_pairs={{0,8},{4,12},{8,0},{12,4},{1,9},{5,13},{9,1},{13,5},{2,10},{6,14},... | collective-permute-start | bytes 1036808 | tf_op jit(solution)/shard_map/ppermute | solution.py:377
  114.9 28.1 %collective-permute-start.5 = (bf16[300,576]{0,1:T(8,128)(2,1)S(1)}, bf16[300,576]{0,1:T(8,128)(2,1)}, u32[]{:S(2)}, u32[]{:S(2)}) collective-permute-start(bf16[300,576]{0,1:T(8,128)(2,1)S(1)} %pad_maximum_fusion.4), channel_id=1, source_target_pairs={{0,4},{4,8},{8,12},{12,0},{1,5},{5,9},{9,13},{13,1},{2,6},{6,10},{... | collective-permute-start | bytes 1036808 | tf_op jit(solution)/shard_map/ppermute | solution.py:377
  143.0 22.8 %all-to-all-start.2 = ((bf16[8,64,1152]{2,1,0:T(8,128)(2,1)}), bf16[8,64,1152]{2,1,0:T(8,128)(2,1)}, u32[]{:S(2)}, u32[]{:S(2)}) async-start(bf16[8,64,1152]{2,1,0:T(8,128)(2,1)} %bitcast.47), calls=%async_computation.2 | async-start | bytes 2359296 | tf_op jit(solution)/shard_map/all_to_all | solution.py:420
Sparse Core Ops, SparseCore 0:
  19.8 62.4 all-gather.6
  112.4 39.7 all-gather.4

commit v2 on v1

--- a/solution.py
+++ b/solution.py
@@ -187,18 +187,18 @@
 
 def piece_copies(place, gathered, weight, sems):
     z = place[0]
-    width = gathered.shape[3]
-    parts = weight.shape[1] // width
+    parts = weight.shape[1] // gathered.shape[3]
     copies = []
-    for y in range(parts):
+    for column in range(0, weight.shape[1], D):
+        y, at = divmod(column, gathered.shape[3])
         for x in range(4):
             for core in range(2):
                 low, count = (0, HALF) if core == 0 else (HALF - 64, 64)
                 for dz in range(2):
                     shard = 2 * x + (z if dz == 0 else 1 - z)
                     row = pl.multiple_of(shard * SHARD + core * HALF, 16)
-                    dst = weight.at[pl.ds(row, count), pl.ds(y * width, width)]
-                    src = gathered.at[(x * parts + y) * 2 + core, dz, pl.ds(low, count), :]
+                    dst = weight.at[pl.ds(row, count), pl.ds(column, D)]
+                    src = gathered.at[(x * parts + y) * 2 + core, dz, pl.ds(low, count), pl.ds(at, D)]
                     copies.append(pltpu.make_async_copy(src, dst, sems.at[len(copies)]))
     return copies
 
@@ -297,7 +297,7 @@
         copy.start()
     rows = x.shape[0]
     R = 256
-    for copy in copies:
+    for copy in copies[:16]:
         copy.wait()
     for b in range(rows // R):
         sl = pl.ds(b * R, R)
@@ -316,6 +316,8 @@
             at[head_rows(h), :] = o[:HD] * (1.0 / o[HD:HD + 1])
 
     loop(HEADS // 2, pair)
+    for copy in copies[16:]:
+        copy.wait()
     for b in range(rows // R):
         sl = pl.ds(b * R, R)
         mixed = x[sl, :].astype(F32) + dot(at[:, sl].T.astype(BF), w[:, D:])
@@ -394,20 +396,17 @@
     gain_t = gains(qk_gains[2], qk_gains[3])
     count = jnp.sum((frame_valid > 0).astype(jnp.int32))
     place = jnp.stack([lax.axis_index("zh"), core, count]).astype(jnp.int32)
-    both1, local, gain_s, gain_t, place = bar((both1, local, gain_s, gain_t, place))
     gathered1 = lax.all_gather(both1, ("x", "y", "c"), axis=0)
-    own, local, w2 = bar((own, local, w2))
+    pair = in_pairs(local, "c", swap(local))
+    own, pair, w2, gain_s, gain_t, place = bar((own, pair, w2, gain_s, gain_t, place))
 
     other = swap(own)
-    swapped = swap(local)
+    besides = lax.ppermute(pair, "zl", SWAP)
     z2 = across(w2)
     after_spatial = spatial(own, other, spatial_qkv, spatial_out, modulation, gain_s)
-    after_spatial, swapped, z2 = bar((after_spatial, swapped, z2))
+    after_spatial, besides, z2 = bar((after_spatial, besides, z2))
 
     rows = lax.all_to_all(after_spatial.reshape(64, 8, D), YZ + XZ, 0, 0, tiled=True).reshape(-1, D)
-    pair = in_pairs(local, "c", swapped)
-    besides = lax.ppermute(pair, "zl", SWAP)
-    rows, besides = bar((rows, besides))
     steps = along_y(in_pairs(pair, "zl", besides))
     _, both2 = bar((rows, jnp.stack([w2, z2])))
     gathered2 = lax.all_gather(both2, ("x", "c"), axis=0)

time: 191 us -> 186 us (0.974)
  waiting for transfers between devices: 50.9 us -> 47.8 us
    all_to_all x1, waiting for transfers between devices: 0.3 us -> 18.6 us  [per_device(): lax.all_to_all(after_spatial.reshape(64, 8, D), YZ + XZ, 0, 0, tiled=True)]
    ppermute x1, waiting for transfers between devices: 16.6 us -> 0.01 us  [per_device(): besides = lax.ppermute(pair, 'zl', SWAP)]
    all_to_all x1, waiting for transfers between devices: 20.5 us -> 15.9 us  [per_device(): own = lax.all_to_all(tokens, YZ, 0, 0, tiled=True).reshape(-1, D)]
    ppermute x2, starting transfers between devices: 4.12 us -> 8.15 us  [across(): return lax.ppermute(v, ('zh', 'zl'), ACROSS)]
    ppermute x2, waiting for transfers between devices: 0.01 us -> 3.69 us  [across(): return lax.ppermute(v, ('zh', 'zl'), ACROSS)]
    ppermute x2, waiting for transfers between devices: 2.63 us -> 0.01 us  [swap(): return lax.ppermute(v, 'c', SWAP)]
    all_to_all x1, starting transfers between devices: 6.32 us -> 4.26 us  [per_device(): lax.all_to_all(after_temporal.reshape(8, 64, D), XZ, 0, 0, tiled=True)]
  transfers between devices with their start and end apart: 13 -> 13, of which waited for: 5 -> 4; matrix products, arithmetic and copies ran while one was open for 8% -> 7% of each run, Pallas kernels for 33% -> 34%
where the time goes in v2:
time: 186 us; the launch traced here: 185 us
  Pallas kernels  79.3 us (43%)
  waiting for transfers between devices  47.8 us (26%)
  starting transfers between devices  30 us (16%)
  between operations  13.7 us (7%)
  other arithmetic  8.27 us (4%)
  local copies, waits for them, and re-layouts  5.66 us (3%)
    pallas_call x1, Pallas kernels, spatial(): pl.pallas_call(functools.partial(spatial_kernel, rows=rows), out_shape=ja...  35.8 us
    pallas_call x1, Pallas kernels, temporal(): pl.pallas_call(functools.partial(temporal_kernel, rows=rows, frames=64),...  26.9 us
    all_to_all x1, waiting for transfers between devices, per_device(): lax.all_to_all(after_spatial.reshape(64, 8, D), YZ + XZ, 0, 0, tiled=True)  18.6 us
    pallas_call x1, Pallas kernels, cross(): pl.pallas_call(cross_kernel, out_shape=jax.ShapeDtypeStruct((8, rows // 8...  16.6 us
    all_to_all x1, waiting for transfers between devices, per_device(): own = lax.all_to_all(tokens, YZ, 0, 0, tiled=True).reshape(-1, D)  15.9 us
    all_to_all x1, waiting for transfers between devices, per_device(): lax.all_to_all(after_temporal.reshape(8, 64, D), XZ, 0, 0, tiled=True)  9.53 us
    all_to_all x1, starting transfers between devices, per_device(): lax.all_to_all(after_spatial.reshape(64, 8, D), YZ + XZ, 0, 0, tiled=True)  8.59 us
    ppermute x2, starting transfers between devices, across(): return lax.ppermute(v, ('zh', 'zl'), ACROSS)  8.15 us
  transfers between devices with their start and end apart: 13, of which 4 were waited for; matrix products, arithmetic and copies ran while one was open for 7% of the time, Pallas kernels for 34%

profile of v2, /device:TPU:8, one launch (start us, length us, event | category | flops | bytes accessed | tf_op | source)
XLA Modules:
  0.0 185.1 jit_solution(11389885106059289015)
XLA Ops:
  6.5 1.0 dynamic_slice.20
  7.5 4.1 %collective-permute-start.4 = (bf16[80,1152]{1,0:T(8,128)(2,1)S(1)}, bf16[80,1152]{1,0:T(8,128)(2,1)S(1)}, u32[]{:S(2)}, u32[]{:S(2)}) collective-permute-start(bf16[80,1152]{1,0:T(8,128)(2,1)S(1)} %dynamic_slice.20), channel_id=1, source_target_pairs={{0,18},{18,0},{2,16},{16,2},{1,19},{19,1},{3,17},{17,3},{4,22},{22... | collective-permute-start | bytes 552968 | tf_op jit(solution)/shard_map/ppermute | solution.py:366
  11.7 0.9 dynamic-slice_bitcast_fusion
  12.6 3.7 %collective-permute-done.4 = bf16[80,1152]{1,0:T(8,128)(2,1)S(1)} collective-permute-done((bf16[80,1152]{1,0:T(8,128)(2,1)S(1)}, bf16[80,1152]{1,0:T(8,128)(2,1)S(1)}, u32[]{:S(2)}, u32[]{:S(2)}) %collective-permute-start.4) | collective-permute-done | bytes 184352 | tf_op jit(solution)/shard_map/ppermute | solution.py:366
  16.3 0.8 pad_maximum_fusion.5
  17.1 4.9 %all-to-all-start = ((bf16[8,64,1152]{2,1,0:T(8,128)(2,1)}), bf16[8,64,1152]{2,1,0:T(8,128)(2,1)S(1)}, u32[]{:S(2)}, u32[]{:S(2)}) async-start(bf16[8,64,1152]{2,1,0:T(8,128)(2,1)} %param.9), calls=%async_computation | async-start | bytes 2359296 | tf_op jit(solution)/shard_map/all_to_all | solution.py:390
  24.7 1.0 constant_dynamic-slice_fusion.4
  25.7 1.3 pad_add_fusion.place
  27.1 15.9 %all-to-all-done = bf16[8,64,1152]{2,1,0:T(8,128)(2,1)S(1)} async-done(((bf16[8,64,1152]{2,1,0:T(8,128)(2,1)}), bf16[8,64,1152]{2,1,0:T(8,128)(2,1)S(1)}, u32[]{:S(2)}, u32[]{:S(2)}) %all-to-all-start) | async-done | bytes 1179680 | tf_op jit(solution)/shard_map/all_to_all | solution.py:390
  43.0 4.0 %collective-permute-start.3 = (bf16[80,2304]{1,0:T(8,128)(2,1)S(1)}, bf16[80,2304]{1,0:T(8,128)(2,1)S(1)}, u32[]{:S(2)}, u32[]{:S(2)}) collective-permute-start(bf16[80,2304]{1,0:T(8,128)(2,1)S(1)} %constant_dynamic-slice_fusion.4), channel_id=1, source_target_pairs={{0,18},{18,0},{2,16},{16,2},{1,19},{19,1},{3,17},{17,3},{4,22},{22... | collective-permute-start | bytes 1105928 | tf_op jit(solution)/shard_map/ppermute | solution.py:366
  47.0 35.8 %spatial.1 = bf16[512,1152]{1,0:T(8,128)(2,1)} custom-call(bf16[512,1152]{1,0:T(8,128)(2,1)} %bitcast.48, bf16[512,1152]{1,0:T(8,128)(2,1)} %collective-permute-done.1.other_hbm, bf16[1152,3456]{1,0:T(8,128)(2,1)} %wqkv_hbm.1, bf16[1152,1152]{1,0:T(8,128)(2,1)} %wout_hbm.1, f32[6,1152]{1,0:T(8,128)} %mod.3, f32[1,1152]{1,0:T(1,128)} %reshape_tile.6.gain), custom_call_target="tpu_custom_call" | custom-call | flops 30000001024 | bytes 20000000 | tf_op jit(solution)/shard_map/spatial/pallas_call | solution.py:165
  82.9 8.6 %all-to-all-start.1 = ((bf16[64,8,1152]{2,1,0:T(8,128)(2,1)}), bf16[64,8,1152]{2,1,0:T(8,128)(2,1)S(1)}, u32[]{:S(2)}, u32[]{:S(2)}) async-start(bf16[64,8,1152]{2,1,0:T(8,128)(2,1)} %bitcast.50), calls=%async_computation.1 | async-start | bytes 2359296 | tf_op jit(solution)/shard_map/all_to_all | solution.py:409
  91.5 0.9 pad_maximum_fusion.2
  92.5 18.6 %all-to-all-done.1 = bf16[64,8,1152]{2,1,0:T(8,128)(2,1)S(1)} async-done(((bf16[64,8,1152]{2,1,0:T(8,128)(2,1)}), bf16[64,8,1152]{2,1,0:T(8,128)(2,1)S(1)}, u32[]{:S(2)}, u32[]{:S(2)}) %all-to-all-start.1) | async-done | bytes 1179680 | tf_op jit(solution)/shard_map/all_to_all | solution.py:409
  111.2 1.4 collective-permute-start.7
  113.0 2.2 %collective-permute-start.5 = (bf16[300,576]{0,1:T(8,128)(2,1)S(1)}, bf16[300,576]{0,1:T(8,128)(2,1)}, u32[]{:S(2)}, u32[]{:S(2)}) collective-permute-start(bf16[300,576]{0,1:T(8,128)(2,1)S(1)} %pad_maximum_fusion.4), channel_id=1, source_target_pairs={{0,4},{4,8},{8,12},{12,0},{1,5},{5,9},{9,13},{13,1},{2,6},{6,10},{... | collective-permute-start | bytes 1036808 | tf_op jit(solution)/shard_map/ppermute | solution.py:379
  115.2 26.9 %temporal.1 = bf16[512,1152]{1,0:T(8,128)(2,1)} custom-call(s32[3]{0:T(128)} %pad_add_fusion.place, bf16[32,2,80,1152]{3,2,1,0:T(8,128)(2,1)} %bitcast.56, bf16[512,1152]{1,0:T(8,128)(2,1)} %bitcast.46, f32[6,1152]{1,0:T(8,128)} %mod.3, f32[1,1152]{1,0:T(1,128)} %reshape_tile.7.gain), custom_call_target="tpu_custom_call" | custom-call | flops 20000000000 | bytes 20000000 | tf_op jit(solution)/shard_map/temporal/pallas_call | solution.py:273
  142.1 4.3 %all-to-all-start.2 = ((bf16[8,64,1152]{2,1,0:T(8,128)(2,1)}), bf16[8,64,1152]{2,1,0:T(8,128)(2,1)}, u32[]{:S(2)}, u32[]{:S(2)}) async-start(bf16[8,64,1152]{2,1,0:T(8,128)(2,1)} %bitcast.49), calls=%async_computation.2 | async-start | bytes 2359296 | tf_op jit(solution)/shard_map/all_to_all | solution.py:419
  146.4 1.4 pad_maximum_fusion
  149.0 0.8 copy.12
  149.9 0.9 pad_maximum_fusion.3.tk
  150.8 1.4 pad_convert_fusion.tvt
  152.2 9.5 %all-to-all-done.2 = bf16[8,64,1152]{2,1,0:T(8,128)(2,1)} async-done(((bf16[8,64,1152]{2,1,0:T(8,128)(2,1)}), bf16[8,64,1152]{2,1,0:T(8,128)(2,1)}, u32[]{:S(2)}, u32[]{:S(2)}) %all-to-all-start.2) | async-done | bytes 1179680 | tf_op jit(solution)/shard_map/all_to_all | solution.py:419
  161.7 16.6 %cross.1 = bf16[8,64,1152]{2,1,0:T(8,128)(2,1)} custom-call(s32[3]{0:T(128)} %pad_add_fusion.place, bf16[8,2,80,2304]{3,2,1,0:T(8,128)(2,1)} %bitcast.57, bf16[512,1152]{1,0:T(8,128)(2,1)} %bitcast.16.x, bf16[304,1152]{1,0:T(8,128)(2,1)} %pad_maximum_fusion.3.tk, f32[1152,304]{1,0:T(8,128)} %pad_convert_fusion.tvt), custom_call_target="tpu_custom_call" | custom-call | flops 20000000000 | bytes 20000000 | tf_op jit(solution)/shard_map/cross/pallas_call | solution.py:332
  (46 shorter events, 4.3 us)
Async XLA Ops:
  6.5 15.6 %copy-start = (bf16[300,1152]{1,0:T(8,128)(2,1)S(1)}, bf16[300,1152]{1,0:T(8,128)(2,1)}, u32[]{:S(2)}) copy-start(bf16[300,1152]{1,0:T(8,128)(2,1)} %param.11) | copy-start | bytes 2073604
  6.5 108.6 %all-gather.7.cloned.1.call-start = ((), (), s32[]{:S(2)}) async-start(), calls=%async_computation.4 | async-start | bytes 12165120 | tf_op jit(solution)/shard_map/all_gather | solution.py:399
  7.5 8.8 %collective-permute-start.4 = (bf16[80,1152]{1,0:T(8,128)(2,1)S(1)}, bf16[80,1152]{1,0:T(8,128)(2,1)S(1)}, u32[]{:S(2)}, u32[]{:S(2)}) collective-permute-start(bf16[80,1152]{1,0:T(8,128)(2,1)S(1)} %dynamic_slice.20), channel_id=1, source_target_pairs={{0,18},{18,0},{2,16},{16,2},{1,19},{19,1},{3,17},{17,3},{4,22},{22... | collective-permute-start | bytes 552968 | tf_op jit(solution)/shard_map/ppermute | solution.py:366
  12.6 9.5 %copy-start.3 = (bf16[1152,2,72]{0,2,1:T(8,128)(2,1)S(1)}, bf16[1152,2,72]{0,2,1:T(8,128)(2,1)}, u32[]{:S(2)}) copy-start(bf16[1152,2,72]{0,2,1:T(8,128)(2,1)} %param.17) | copy-start | bytes 995332
  17.1 5.5 %copy-start.4 = (f32[4,72]{1,0:T(4,128)S(1)}, f32[4,72]{1,0:T(4,128)}, u32[]{:S(2)}) copy-start(f32[4,72]{1,0:T(4,128)} %param.13) | copy-start | bytes 3460
  17.1 6.9 %copy-start.5 = (s32[64]{0:T(128)S(1)}, s32[64]{0:T(128)}, u32[]{:S(2)}) copy-start(s32[64]{0:T(128)} %param.10) | copy-start | bytes 772
  17.1 25.8 %all-to-all-start = ((bf16[8,64,1152]{2,1,0:T(8,128)(2,1)}), bf16[8,64,1152]{2,1,0:T(8,128)(2,1)S(1)}, u32[]{:S(2)}, u32[]{:S(2)}) async-start(bf16[8,64,1152]{2,1,0:T(8,128)(2,1)} %param.9), calls=%async_computation | async-start | bytes 2359296 | tf_op jit(solution)/shard_map/all_to_all | solution.py:390
  22.5 4.5 %collective-permute-start = (bf16[300,144]{0,1:T(8,128)(2,1)S(1)}, bf16[300,144]{0,1:T(8,128)(2,1)S(1)}, u32[]{:S(2)}, u32[]{:S(2)}) collective-permute-start(bf16[300,144]{0,1:T(8,128)(2,1)S(1)} %convolution_convert_fusion), channel_id=1, source_target_pairs={{0,1},{1,0},{2,3},{3,2},{4,5},{5,4},{6,7},{7,6},{8,9},{9,8},{10,11... | collective-permute-start | bytes 259208 | tf_op jit(solution)/shard_map/ppermute | solution.py:370
  43.0 4.0 %copy-start.2 = (bf16[8,64,1152]{2,1,0:T(8,128)(2,1)}, bf16[8,64,1152]{2,1,0:T(8,128)(2,1)S(1)}, u32[]{:S(2)}) copy-start(bf16[8,64,1152]{2,1,0:T(8,128)(2,1)S(1)} %all-to-all-done) | copy-start | bytes 3538948
  43.0 4.0 %collective-permute-start.1 = (bf16[512,1152]{1,0:T(8,128)(2,1)S(1)}, bf16[512,1152]{1,0:T(8,128)(2,1)}, u32[]{:S(2)}, u32[]{:S(2)}) collective-permute-start(bf16[512,1152]{1,0:T(8,128)(2,1)S(1)} %bitcast.47), channel_id=1, source_target_pairs={{0,1},{1,0},{2,3},{3,2},{4,5},{5,4},{6,7},{7,6},{8,9},{9,8},{10,11... | collective-permute-start | bytes 3538952 | tf_op jit(solution)/shard_map/ppermute | solution.py:370
  43.0 39.9 %collective-permute-start.2 = (bf16[300,288]{0,1:T(8,128)(2,1)S(1)}, bf16[300,288]{0,1:T(8,128)(2,1)S(1)}, u32[]{:S(2)}, u32[]{:S(2)}) collective-permute-start(bf16[300,288]{0,1:T(8,128)(2,1)S(1)} %pad_maximum_fusion.6), channel_id=1, source_target_pairs={{0,2},{2,0},{1,3},{3,1},{4,6},{6,4},{5,7},{7,5},{8,10},{10,8},{9,1... | collective-permute-start | bytes 518408 | tf_op jit(solution)/shard_map/ppermute | solution.py:404
  43.0 39.9 %collective-permute-start.3 = (bf16[80,2304]{1,0:T(8,128)(2,1)S(1)}, bf16[80,2304]{1,0:T(8,128)(2,1)S(1)}, u32[]{:S(2)}, u32[]{:S(2)}) collective-permute-start(bf16[80,2304]{1,0:T(8,128)(2,1)S(1)} %constant_dynamic-slice_fusion.4), channel_id=1, source_target_pairs={{0,18},{18,0},{2,16},{16,2},{1,19},{19,1},{3,17},{17,3},{4,22},{22... | collective-permute-start | bytes 1105928 | tf_op jit(solution)/shard_map/ppermute | solution.py:366
  82.9 28.2 %all-to-all-start.1 = ((bf16[64,8,1152]{2,1,0:T(8,128)(2,1)}), bf16[64,8,1152]{2,1,0:T(8,128)(2,1)S(1)}, u32[]{:S(2)}, u32[]{:S(2)}) async-start(bf16[64,8,1152]{2,1,0:T(8,128)(2,1)} %bitcast.50), calls=%async_computation.1 | async-start | bytes 2359296 | tf_op jit(solution)/shard_map/all_to_all | solution.py:409
  91.5 60.7 %all-gather.5.cloned.1.call-start = ((), (), s32[]{:S(2)}) async-start(), calls=%async_computation.3 | async-start | bytes 6635520 | tf_op jit(solution)/shard_map/all_gather | solution.py:412
  111.0 4.1 %copy-start.1 = (bf16[64,8,1152]{2,1,0:T(8,128)(2,1)}, bf16[64,8,1152]{2,1,0:T(8,128)(2,1)S(1)}, u32[]{:S(2)}) copy-start(bf16[64,8,1152]{2,1,0:T(8,128)(2,1)S(1)} %all-to-all-done.1) | copy-start | bytes 3538948
  111.2 30.9 %collective-permute-start.7 = (bf16[300,576]{0,1:T(8,128)(2,1)S(1)}, bf16[300,576]{0,1:T(8,128)(2,1)S(1)}, u32[]{:S(2)}, u32[]{:S(2)}) collective-permute-start(bf16[300,576]{0,1:T(8,128)(2,1)S(1)} %pad_maximum_fusion.4), channel_id=1, source_target_pairs={{0,12},{4,0},{8,4},{12,8},{1,13},{5,1},{9,5},{13,9},{2,14},{6,2},{... | collective-permute-start | bytes 1036808 | tf_op jit(solution)/shard_map/ppermute | solution.py:379
  112.6 29.5 %collective-permute-start.6 = (bf16[300,576]{0,1:T(8,128)(2,1)S(1)}, bf16[300,576]{0,1:T(8,128)(2,1)S(1)}, u32[]{:S(2)}, u32[]{:S(2)}) collective-permute-start(bf16[300,576]{0,1:T(8,128)(2,1)S(1)} %pad_maximum_fusion.4), channel_id=1, source_target_pairs={{0,8},{4,12},{8,0},{12,4},{1,9},{5,13},{9,1},{13,5},{2,10},{6,14},... | collective-permute-start | bytes 1036808 | tf_op jit(solution)/shard_map/ppermute | solution.py:379
  113.0 29.2 %collective-permute-start.5 = (bf16[300,576]{0,1:T(8,128)(2,1)S(1)}, bf16[300,576]{0,1:T(8,128)(2,1)}, u32[]{:S(2)}, u32[]{:S(2)}) collective-permute-start(bf16[300,576]{0,1:T(8,128)(2,1)S(1)} %pad_maximum_fusion.4), channel_id=1, source_target_pairs={{0,4},{4,8},{8,12},{12,0},{1,5},{5,9},{9,13},{13,1},{2,6},{6,10},{... | collective-permute-start | bytes 1036808 | tf_op jit(solution)/shard_map/ppermute | solution.py:379
  142.1 19.6 %all-to-all-start.2 = ((bf16[8,64,1152]{2,1,0:T(8,128)(2,1)}), bf16[8,64,1152]{2,1,0:T(8,128)(2,1)}, u32[]{:S(2)}, u32[]{:S(2)}) async-start(bf16[8,64,1152]{2,1,0:T(8,128)(2,1)} %bitcast.49), calls=%async_computation.2 | async-start | bytes 2359296 | tf_op jit(solution)/shard_map/all_to_all | solution.py:419
Sparse Core Ops, SparseCore 0:
  17.2 64.9 all-gather.6
  111.2 36.0 all-gather.4

commit v3 on v2

--- a/solution.py
+++ b/solution.py
@@ -134,15 +134,15 @@
     loop(rows // R, project)
 
     def run(shifted):
-        def pair(i):
-            for h in (2 * i, 2 * i + 1):
+        def heads(i):
+            for h in [i] if shifted else [4 * i + j for j in range(4)]:
                 start, _ = window_of(h)
                 q = query_of(qt, h, True)
                 p = softmax(dot(k[:, pl.ds(start, WIN)], q), shifted)
                 o = dot(values_of(vt, h, slice(None)), p)
                 at[head_rows(h), :] = o[:HD] * (1.0 / o[HD:HD + 1])
 
-        loop(HEADS // 2, pair)
+        loop(HEADS if shifted else HEADS // 4, heads)
 
     guarded(gain, run)
 
@@ -238,8 +238,8 @@
     bias = jnp.where((row // frames == query) & (frame < place[2]), 0.0, -1e30)
 
     def run(shifted):
-        def pair(i):
-            for h in (2 * i, 2 * i + 1):
+        def heads(i):
+            for h in [i] if shifted else [4 * i + j for j in range(4)]:
                 start, _ = window_of(h)
                 q = query_of(qt, h, True)
                 for b in range(rows // R):
@@ -248,7 +248,7 @@
                     o = dot(values_of(vt, h, sl), softmax(s, shifted))
                     at[head_rows(h), sl] = o[:HD] * (1.0 / o[HD:HD + 1])
 
-        loop(HEADS // 2, pair)
+        loop(HEADS if shifted else HEADS // 4, heads)
 
     guarded(gain, run)
     for copy in copies[48:]:
@@ -306,8 +306,8 @@
     lane = lax.broadcasted_iota(jnp.int32, (8, TPAD), 1)
     ones = (lane < TEXT).astype(F32).astype(BF)
 
-    def pair(i):
-        for h in (2 * i, 2 * i + 1):
+    def heads(i):
+        for h in [4 * i + j for j in range(4)]:
             start, _ = window_of(h)
             q = query_of(qt, h, False)
             p = softmax(dot(tk[:, pl.ds(start, WIN)], q), True)
@@ -315,7 +315,7 @@
             o = dot(v, p)
             at[head_rows(h), :] = o[:HD] * (1.0 / o[HD:HD + 1])
 
-    loop(HEADS // 2, pair)
+    loop(HEADS // 4, heads)
     for copy in copies[16:]:
         copy.wait()
     for b in range(rows // R):

time: 186 us -> 188 us (1.011)
  Pallas kernels: 79.3 us -> 81.2 us
  transfers between devices with their start and end apart: 13 -> 13, of which waited for: 4 -> 4; matrix products, arithmetic and copies ran while one was open for 7% -> 7% of each run, Pallas kernels for 34% -> 35%
where the time goes in v3:
time: 188 us; the launch traced here: 187 us
  Pallas kernels  81.2 us (43%)
  waiting for transfers between devices  47.8 us (25%)
  starting transfers between devices  30 us (16%)
  between operations  13.7 us (7%)
  other arithmetic  8.27 us (4%)
  local copies, waits for them, and re-layouts  5.66 us (3%)
    pallas_call x1, Pallas kernels, spatial(): pl.pallas_call(functools.partial(spatial_kernel, rows=rows), out_shape=ja...  37.1 us
    pallas_call x1, Pallas kernels, temporal(): pl.pallas_call(functools.partial(temporal_kernel, rows=rows, frames=64),...  28.3 us
    all_to_all x1, waiting for transfers between devices, per_device(): lax.all_to_all(after_spatial.reshape(64, 8, D), YZ + XZ, 0, 0, tiled=True)  18.6 us
    all_to_all x1, waiting for transfers between devices, per_device(): own = lax.all_to_all(tokens, YZ, 0, 0, tiled=True).reshape(-1, D)  15.9 us
    pallas_call x1, Pallas kernels, cross(): pl.pallas_call(cross_kernel, out_shape=jax.ShapeDtypeStruct((8, rows // 8...  15.8 us
    all_to_all x1, waiting for transfers between devices, per_device(): lax.all_to_all(after_temporal.reshape(8, 64, D), XZ, 0, 0, tiled=True)  9.53 us
    all_to_all x1, starting transfers between devices, per_device(): lax.all_to_all(after_spatial.reshape(64, 8, D), YZ + XZ, 0, 0, tiled=True)  8.6 us
    ppermute x2, starting transfers between devices, across(): return lax.ppermute(v, ('zh', 'zl'), ACROSS)  8.15 us
  transfers between devices with their start and end apart: 13, of which 4 were waited for; matrix products, arithmetic and copies ran while one was open for 7% of the time, Pallas kernels for 35%

profile of v3, /device:TPU:8, one launch (start us, length us, event | category | flops | bytes accessed | tf_op | source)
XLA Modules:
  0.0 187.1 jit_solution(3382378880274708511)
XLA Ops:
  6.5 1.0 dynamic_slice.20
  7.5 4.1 %collective-permute-start.4 = (bf16[80,1152]{1,0:T(8,128)(2,1)S(1)}, bf16[80,1152]{1,0:T(8,128)(2,1)S(1)}, u32[]{:S(2)}, u32[]{:S(2)}) collective-permute-start(bf16[80,1152]{1,0:T(8,128)(2,1)S(1)} %dynamic_slice.20), channel_id=1, source_target_pairs={{0,18},{18,0},{2,16},{16,2},{1,19},{19,1},{3,17},{17,3},{4,22},{22... | collective-permute-start | bytes 552968 | tf_op jit(solution)/shard_map/ppermute | solution.py:366
  11.7 0.9 dynamic-slice_bitcast_fusion
  12.6 3.7 %collective-permute-done.4 = bf16[80,1152]{1,0:T(8,128)(2,1)S(1)} collective-permute-done((bf16[80,1152]{1,0:T(8,128)(2,1)S(1)}, bf16[80,1152]{1,0:T(8,128)(2,1)S(1)}, u32[]{:S(2)}, u32[]{:S(2)}) %collective-permute-start.4) | collective-permute-done | bytes 184352 | tf_op jit(solution)/shard_map/ppermute | solution.py:366
  16.3 0.8 pad_maximum_fusion.5
  17.1 4.9 %all-to-all-start = ((bf16[8,64,1152]{2,1,0:T(8,128)(2,1)}), bf16[8,64,1152]{2,1,0:T(8,128)(2,1)S(1)}, u32[]{:S(2)}, u32[]{:S(2)}) async-start(bf16[8,64,1152]{2,1,0:T(8,128)(2,1)} %param.9), calls=%async_computation | async-start | bytes 2359296 | tf_op jit(solution)/shard_map/all_to_all | solution.py:390
  24.7 1.0 constant_dynamic-slice_fusion.4
  25.7 1.3 pad_add_fusion.place
  27.1 15.9 %all-to-all-done = bf16[8,64,1152]{2,1,0:T(8,128)(2,1)S(1)} async-done(((bf16[8,64,1152]{2,1,0:T(8,128)(2,1)}), bf16[8,64,1152]{2,1,0:T(8,128)(2,1)S(1)}, u32[]{:S(2)}, u32[]{:S(2)}) %all-to-all-start) | async-done | bytes 1179680 | tf_op jit(solution)/shard_map/all_to_all | solution.py:390
  43.0 4.0 %collective-permute-start.3 = (bf16[80,2304]{1,0:T(8,128)(2,1)S(1)}, bf16[80,2304]{1,0:T(8,128)(2,1)S(1)}, u32[]{:S(2)}, u32[]{:S(2)}) collective-permute-start(bf16[80,2304]{1,0:T(8,128)(2,1)S(1)} %constant_dynamic-slice_fusion.4), channel_id=1, source_target_pairs={{0,18},{18,0},{2,16},{16,2},{1,19},{19,1},{3,17},{17,3},{4,22},{22... | collective-permute-start | bytes 1105928 | tf_op jit(solution)/shard_map/ppermute | solution.py:366
  47.0 37.1 %spatial.1 = bf16[512,1152]{1,0:T(8,128)(2,1)} custom-call(bf16[512,1152]{1,0:T(8,128)(2,1)} %bitcast.48, bf16[512,1152]{1,0:T(8,128)(2,1)} %collective-permute-done.1.other_hbm, bf16[1152,3456]{1,0:T(8,128)(2,1)} %wqkv_hbm.1, bf16[1152,1152]{1,0:T(8,128)(2,1)} %wout_hbm.1, f32[6,1152]{1,0:T(8,128)} %mod.3, f32[1,1152]{1,0:T(1,128)} %reshape_tile.6.gain), custom_call_target="tpu_custom_call" | custom-call | flops 30000001024 | bytes 20000000 | tf_op jit(solution)/shard_map/spatial/pallas_call | solution.py:165
  84.2 8.6 %all-to-all-start.1 = ((bf16[64,8,1152]{2,1,0:T(8,128)(2,1)}), bf16[64,8,1152]{2,1,0:T(8,128)(2,1)S(1)}, u32[]{:S(2)}, u32[]{:S(2)}) async-start(bf16[64,8,1152]{2,1,0:T(8,128)(2,1)} %bitcast.50), calls=%async_computation.1 | async-start | bytes 2359296 | tf_op jit(solution)/shard_map/all_to_all | solution.py:409
  92.9 0.9 pad_maximum_fusion.2
  93.8 18.6 %all-to-all-done.1 = bf16[64,8,1152]{2,1,0:T(8,128)(2,1)S(1)} async-done(((bf16[64,8,1152]{2,1,0:T(8,128)(2,1)}), bf16[64,8,1152]{2,1,0:T(8,128)(2,1)S(1)}, u32[]{:S(2)}, u32[]{:S(2)}) %all-to-all-start.1) | async-done | bytes 1179680 | tf_op jit(solution)/shard_map/all_to_all | solution.py:409
  112.5 1.4 collective-permute-start.7
  114.3 2.2 %collective-permute-start.5 = (bf16[300,576]{0,1:T(8,128)(2,1)S(1)}, bf16[300,576]{0,1:T(8,128)(2,1)}, u32[]{:S(2)}, u32[]{:S(2)}) collective-permute-start(bf16[300,576]{0,1:T(8,128)(2,1)S(1)} %pad_maximum_fusion.4), channel_id=1, source_target_pairs={{0,4},{4,8},{8,12},{12,0},{1,5},{5,9},{9,13},{13,1},{2,6},{6,10},{... | collective-permute-start | bytes 1036808 | tf_op jit(solution)/shard_map/ppermute | solution.py:379
  116.5 28.3 %temporal.1 = bf16[512,1152]{1,0:T(8,128)(2,1)} custom-call(s32[3]{0:T(128)} %pad_add_fusion.place, bf16[32,2,80,1152]{3,2,1,0:T(8,128)(2,1)} %bitcast.56, bf16[512,1152]{1,0:T(8,128)(2,1)} %bitcast.46, f32[6,1152]{1,0:T(8,128)} %mod.3, f32[1,1152]{1,0:T(1,128)} %reshape_tile.7.gain), custom_call_target="tpu_custom_call" | custom-call | flops 20000000000 | bytes 20000000 | tf_op jit(solution)/shard_map/temporal/pallas_call | solution.py:273
  144.8 4.3 %all-to-all-start.2 = ((bf16[8,64,1152]{2,1,0:T(8,128)(2,1)}), bf16[8,64,1152]{2,1,0:T(8,128)(2,1)}, u32[]{:S(2)}, u32[]{:S(2)}) async-start(bf16[8,64,1152]{2,1,0:T(8,128)(2,1)} %bitcast.49), calls=%async_computation.2 | async-start | bytes 2359296 | tf_op jit(solution)/shard_map/all_to_all | solution.py:419
  149.1 1.4 pad_maximum_fusion
  151.7 0.8 copy.12
  152.6 0.9 pad_maximum_fusion.3.tk
  153.5 1.4 pad_convert_fusion.tvt
  154.9 9.5 %all-to-all-done.2 = bf16[8,64,1152]{2,1,0:T(8,128)(2,1)} async-done(((bf16[8,64,1152]{2,1,0:T(8,128)(2,1)}), bf16[8,64,1152]{2,1,0:T(8,128)(2,1)}, u32[]{:S(2)}, u32[]{:S(2)}) %all-to-all-start.2) | async-done | bytes 1179680 | tf_op jit(solution)/shard_map/all_to_all | solution.py:419
  164.4 15.8 %cross.1 = bf16[8,64,1152]{2,1,0:T(8,128)(2,1)} custom-call(s32[3]{0:T(128)} %pad_add_fusion.place, bf16[8,2,80,2304]{3,2,1,0:T(8,128)(2,1)} %bitcast.57, bf16[512,1152]{1,0:T(8,128)(2,1)} %bitcast.16.x, bf16[304,1152]{1,0:T(8,128)(2,1)} %pad_maximum_fusion.3.tk, f32[1152,304]{1,0:T(8,128)} %pad_convert_fusion.tvt), custom_call_target="tpu_custom_call" | custom-call | flops 20000000000 | bytes 20000000 | tf_op jit(solution)/shard_map/cross/pallas_call | solution.py:332
  (46 shorter events, 4.3 us)
Async XLA Ops:
  6.5 15.6 %copy-start = (bf16[300,1152]{1,0:T(8,128)(2,1)S(1)}, bf16[300,1152]{1,0:T(8,128)(2,1)}, u32[]{:S(2)}) copy-start(bf16[300,1152]{1,0:T(8,128)(2,1)} %param.11) | copy-start | bytes 2073604
  6.5 110.0 %all-gather.7.cloned.1.call-start = ((), (), s32[]{:S(2)}) async-start(), calls=%async_computation.4 | async-start | bytes 12165120 | tf_op jit(solution)/shard_map/all_gather | solution.py:399
  7.5 8.8 %collective-permute-start.4 = (bf16[80,1152]{1,0:T(8,128)(2,1)S(1)}, bf16[80,1152]{1,0:T(8,128)(2,1)S(1)}, u32[]{:S(2)}, u32[]{:S(2)}) collective-permute-start(bf16[80,1152]{1,0:T(8,128)(2,1)S(1)} %dynamic_slice.20), channel_id=1, source_target_pairs={{0,18},{18,0},{2,16},{16,2},{1,19},{19,1},{3,17},{17,3},{4,22},{22... | collective-permute-start | bytes 552968 | tf_op jit(solution)/shard_map/ppermute | solution.py:366
  12.6 9.5 %copy-start.3 = (bf16[1152,2,72]{0,2,1:T(8,128)(2,1)S(1)}, bf16[1152,2,72]{0,2,1:T(8,128)(2,1)}, u32[]{:S(2)}) copy-start(bf16[1152,2,72]{0,2,1:T(8,128)(2,1)} %param.17) | copy-start | bytes 995332
  17.1 5.5 %copy-start.4 = (f32[4,72]{1,0:T(4,128)S(1)}, f32[4,72]{1,0:T(4,128)}, u32[]{:S(2)}) copy-start(f32[4,72]{1,0:T(4,128)} %param.13) | copy-start | bytes 3460
  17.1 6.9 %copy-start.5 = (s32[64]{0:T(128)S(1)}, s32[64]{0:T(128)}, u32[]{:S(2)}) copy-start(s32[64]{0:T(128)} %param.10) | copy-start | bytes 772
  17.1 25.8 %all-to-all-start = ((bf16[8,64,1152]{2,1,0:T(8,128)(2,1)}), bf16[8,64,1152]{2,1,0:T(8,128)(2,1)S(1)}, u32[]{:S(2)}, u32[]{:S(2)}) async-start(bf16[8,64,1152]{2,1,0:T(8,128)(2,1)} %param.9), calls=%async_computation | async-start | bytes 2359296 | tf_op jit(solution)/shard_map/all_to_all | solution.py:390
  22.5 4.5 %collective-permute-start = (bf16[300,144]{0,1:T(8,128)(2,1)S(1)}, bf16[300,144]{0,1:T(8,128)(2,1)S(1)}, u32[]{:S(2)}, u32[]{:S(2)}) collective-permute-start(bf16[300,144]{0,1:T(8,128)(2,1)S(1)} %convolution_convert_fusion), channel_id=1, source_target_pairs={{0,1},{1,0},{2,3},{3,2},{4,5},{5,4},{6,7},{7,6},{8,9},{9,8},{10,11... | collective-permute-start | bytes 259208 | tf_op jit(solution)/shard_map/ppermute | solution.py:370
  43.0 4.0 %copy-start.2 = (bf16[8,64,1152]{2,1,0:T(8,128)(2,1)}, bf16[8,64,1152]{2,1,0:T(8,128)(2,1)S(1)}, u32[]{:S(2)}) copy-start(bf16[8,64,1152]{2,1,0:T(8,128)(2,1)S(1)} %all-to-all-done) | copy-start | bytes 3538948
  43.0 4.0 %collective-permute-start.1 = (bf16[512,1152]{1,0:T(8,128)(2,1)S(1)}, bf16[512,1152]{1,0:T(8,128)(2,1)}, u32[]{:S(2)}, u32[]{:S(2)}) collective-permute-start(bf16[512,1152]{1,0:T(8,128)(2,1)S(1)} %bitcast.47), channel_id=1, source_target_pairs={{0,1},{1,0},{2,3},{3,2},{4,5},{5,4},{6,7},{7,6},{8,9},{9,8},{10,11... | collective-permute-start | bytes 3538952 | tf_op jit(solution)/shard_map/ppermute | solution.py:370
  43.0 41.2 %collective-permute-start.2 = (bf16[300,288]{0,1:T(8,128)(2,1)S(1)}, bf16[300,288]{0,1:T(8,128)(2,1)S(1)}, u32[]{:S(2)}, u32[]{:S(2)}) collective-permute-start(bf16[300,288]{0,1:T(8,128)(2,1)S(1)} %pad_maximum_fusion.6), channel_id=1, source_target_pairs={{0,2},{2,0},{1,3},{3,1},{4,6},{6,4},{5,7},{7,5},{8,10},{10,8},{9,1... | collective-permute-start | bytes 518408 | tf_op jit(solution)/shard_map/ppermute | solution.py:404
  43.0 41.2 %collective-permute-start.3 = (bf16[80,2304]{1,0:T(8,128)(2,1)S(1)}, bf16[80,2304]{1,0:T(8,128)(2,1)S(1)}, u32[]{:S(2)}, u32[]{:S(2)}) collective-permute-start(bf16[80,2304]{1,0:T(8,128)(2,1)S(1)} %constant_dynamic-slice_fusion.4), channel_id=1, source_target_pairs={{0,18},{18,0},{2,16},{16,2},{1,19},{19,1},{3,17},{17,3},{4,22},{22... | collective-permute-start | bytes 1105928 | tf_op jit(solution)/shard_map/ppermute | solution.py:366
  84.2 28.2 %all-to-all-start.1 = ((bf16[64,8,1152]{2,1,0:T(8,128)(2,1)}), bf16[64,8,1152]{2,1,0:T(8,128)(2,1)S(1)}, u32[]{:S(2)}, u32[]{:S(2)}) async-start(bf16[64,8,1152]{2,1,0:T(8,128)(2,1)} %bitcast.50), calls=%async_computation.1 | async-start | bytes 2359296 | tf_op jit(solution)/shard_map/all_to_all | solution.py:409
  92.8 62.0 %all-gather.5.cloned.1.call-start = ((), (), s32[]{:S(2)}) async-start(), calls=%async_computation.3 | async-start | bytes 6635520 | tf_op jit(solution)/shard_map/all_gather | solution.py:412
  112.4 4.1 %copy-start.1 = (bf16[64,8,1152]{2,1,0:T(8,128)(2,1)}, bf16[64,8,1152]{2,1,0:T(8,128)(2,1)S(1)}, u32[]{:S(2)}) copy-start(bf16[64,8,1152]{2,1,0:T(8,128)(2,1)S(1)} %all-to-all-done.1) | copy-start | bytes 3538948
  112.5 32.2 %collective-permute-start.7 = (bf16[300,576]{0,1:T(8,128)(2,1)S(1)}, bf16[300,576]{0,1:T(8,128)(2,1)S(1)}, u32[]{:S(2)}, u32[]{:S(2)}) collective-permute-start(bf16[300,576]{0,1:T(8,128)(2,1)S(1)} %pad_maximum_fusion.4), channel_id=1, source_target_pairs={{0,12},{4,0},{8,4},{12,8},{1,13},{5,1},{9,5},{13,9},{2,14},{6,2},{... | collective-permute-start | bytes 1036808 | tf_op jit(solution)/shard_map/ppermute | solution.py:379
  114.0 30.8 %collective-permute-start.6 = (bf16[300,576]{0,1:T(8,128)(2,1)S(1)}, bf16[300,576]{0,1:T(8,128)(2,1)S(1)}, u32[]{:S(2)}, u32[]{:S(2)}) collective-permute-start(bf16[300,576]{0,1:T(8,128)(2,1)S(1)} %pad_maximum_fusion.4), channel_id=1, source_target_pairs={{0,8},{4,12},{8,0},{12,4},{1,9},{5,13},{9,1},{13,5},{2,10},{6,14},... | collective-permute-start | bytes 1036808 | tf_op jit(solution)/shard_map/ppermute | solution.py:379
  114.3 30.5 %collective-permute-start.5 = (bf16[300,576]{0,1:T(8,128)(2,1)S(1)}, bf16[300,576]{0,1:T(8,128)(2,1)}, u32[]{:S(2)}, u32[]{:S(2)}) collective-permute-start(bf16[300,576]{0,1:T(8,128)(2,1)S(1)} %pad_maximum_fusion.4), channel_id=1, source_target_pairs={{0,4},{4,8},{8,12},{12,0},{1,5},{5,9},{9,13},{13,1},{2,6},{6,10},{... | collective-permute-start | bytes 1036808 | tf_op jit(solution)/shard_map/ppermute | solution.py:379
  144.8 19.6 %all-to-all-start.2 = ((bf16[8,64,1152]{2,1,0:T(8,128)(2,1)}), bf16[8,64,1152]{2,1,0:T(8,128)(2,1)}, u32[]{:S(2)}, u32[]{:S(2)}) async-start(bf16[8,64,1152]{2,1,0:T(8,128)(2,1)} %bitcast.49), calls=%async_computation.2 | async-start | bytes 2359296 | tf_op jit(solution)/shard_map/all_to_all | solution.py:419
Sparse Core Ops, SparseCore 0:
  17.2 64.9 all-gather.6
  112.5 36.0 all-gather.4

commit v4 on v3

--- a/solution.py
+++ b/solution.py
@@ -321,10 +321,11 @@
     for b in range(rows // R):
         sl = pl.ds(b * R, R)
         mixed = x[sl, :].astype(F32) + dot(at[:, sl].T.astype(BF), w[:, D:])
-        for g in range(R // 64):
+        for g in range(0, R // 64, 2):
             for f in range(8):
-                low = g * 64 + f * 8
-                out[f, pl.ds((b * (R // 64) + g) * 8, 8), :] = mixed[low:low + 8, :].astype(BF)
+                low, high = g * 64 + f * 8, (g + 1) * 64 + f * 8
+                two = jnp.concatenate([mixed[low:low + 8, :], mixed[high:high + 8, :]], 0)
+                out[f, pl.ds((b * (R // 64) + g) * 8, 16), :] = two.astype(BF)
 
 
 def cross(place, gathered, x, tk, tvt):

time: 188 us -> 188 us (level)
  no operation moved by 1% of the time
where the time goes in v4:
time: 188 us; the launch traced here: 187 us
  Pallas kernels  81.2 us (43%)
  waiting for transfers between devices  47.8 us (25%)
  starting transfers between devices  30 us (16%)
  between operations  13.7 us (7%)
  other arithmetic  8.27 us (4%)
  local copies, waits for them, and re-layouts  5.66 us (3%)
    pallas_call x1, Pallas kernels, spatial(): pl.pallas_call(functools.partial(spatial_kernel, rows=rows), out_shape=ja...  37.1 us
    pallas_call x1, Pallas kernels, temporal(): pl.pallas_call(functools.partial(temporal_kernel, rows=rows, frames=64),...  28.3 us
    all_to_all x1, waiting for transfers between devices, per_device(): lax.all_to_all(after_spatial.reshape(64, 8, D), YZ + XZ, 0, 0, tiled=True)  18.6 us
    all_to_all x1, waiting for transfers between devices, per_device(): own = lax.all_to_all(tokens, YZ, 0, 0, tiled=True).reshape(-1, D)  15.9 us
    pallas_call x1, Pallas kernels, cross(): pl.pallas_call(cross_kernel, out_shape=jax.ShapeDtypeStruct((8, rows // 8...  15.8 us
    all_to_all x1, waiting for transfers between devices, per_device(): lax.all_to_all(after_temporal.reshape(8, 64, D), XZ, 0, 0, tiled=True)  9.53 us
    all_to_all x1, starting transfers between devices, per_device(): lax.all_to_all(after_spatial.reshape(64, 8, D), YZ + XZ, 0, 0, tiled=True)  8.6 us
    ppermute x2, starting transfers between devices, across(): return lax.ppermute(v, ('zh', 'zl'), ACROSS)  8.15 us
  transfers between devices with their start and end apart: 13, of which 4 were waited for; matrix products, arithmetic and copies ran while one was open for 7% of the time, Pallas kernels for 35%

profile of v4, /device:TPU:8, one launch (start us, length us, event | category | flops | bytes accessed | tf_op | source)
XLA Modules:
  0.0 187.1 jit_solution(3382378880274708511)
XLA Ops:
  6.5 1.0 dynamic_slice.20
  7.5 4.1 %collective-permute-start.4 = (bf16[80,1152]{1,0:T(8,128)(2,1)S(1)}, bf16[80,1152]{1,0:T(8,128)(2,1)S(1)}, u32[]{:S(2)}, u32[]{:S(2)}) collective-permute-start(bf16[80,1152]{1,0:T(8,128)(2,1)S(1)} %dynamic_slice.20), channel_id=1, source_target_pairs={{0,18},{18,0},{2,16},{16,2},{1,19},{19,1},{3,17},{17,3},{4,22},{22... | collective-permute-start | bytes 552968 | tf_op jit(solution)/shard_map/ppermute | solution.py:367
  11.7 0.9 dynamic-slice_bitcast_fusion
  12.6 3.7 %collective-permute-done.4 = bf16[80,1152]{1,0:T(8,128)(2,1)S(1)} collective-permute-done((bf16[80,1152]{1,0:T(8,128)(2,1)S(1)}, bf16[80,1152]{1,0:T(8,128)(2,1)S(1)}, u32[]{:S(2)}, u32[]{:S(2)}) %collective-permute-start.4) | collective-permute-done | bytes 184352 | tf_op jit(solution)/shard_map/ppermute | solution.py:367
  16.3 0.8 pad_maximum_fusion.5
  17.1 4.9 %all-to-all-start = ((bf16[8,64,1152]{2,1,0:T(8,128)(2,1)}), bf16[8,64,1152]{2,1,0:T(8,128)(2,1)S(1)}, u32[]{:S(2)}, u32[]{:S(2)}) async-start(bf16[8,64,1152]{2,1,0:T(8,128)(2,1)} %param.9), calls=%async_computation | async-start | bytes 2359296 | tf_op jit(solution)/shard_map/all_to_all | solution.py:391
  24.7 1.0 constant_dynamic-slice_fusion.4
  25.7 1.3 pad_add_fusion.place
  27.1 15.9 %all-to-all-done = bf16[8,64,1152]{2,1,0:T(8,128)(2,1)S(1)} async-done(((bf16[8,64,1152]{2,1,0:T(8,128)(2,1)}), bf16[8,64,1152]{2,1,0:T(8,128)(2,1)S(1)}, u32[]{:S(2)}, u32[]{:S(2)}) %all-to-all-start) | async-done | bytes 1179680 | tf_op jit(solution)/shard_map/all_to_all | solution.py:391
  43.0 4.0 %collective-permute-start.3 = (bf16[80,2304]{1,0:T(8,128)(2,1)S(1)}, bf16[80,2304]{1,0:T(8,128)(2,1)S(1)}, u32[]{:S(2)}, u32[]{:S(2)}) collective-permute-start(bf16[80,2304]{1,0:T(8,128)(2,1)S(1)} %constant_dynamic-slice_fusion.4), channel_id=1, source_target_pairs={{0,18},{18,0},{2,16},{16,2},{1,19},{19,1},{3,17},{17,3},{4,22},{22... | collective-permute-start | bytes 1105928 | tf_op jit(solution)/shard_map/ppermute | solution.py:367
  47.0 37.1 %spatial.1 = bf16[512,1152]{1,0:T(8,128)(2,1)} custom-call(bf16[512,1152]{1,0:T(8,128)(2,1)} %bitcast.48, bf16[512,1152]{1,0:T(8,128)(2,1)} %collective-permute-done.1.other_hbm, bf16[1152,3456]{1,0:T(8,128)(2,1)} %wqkv_hbm.1, bf16[1152,1152]{1,0:T(8,128)(2,1)} %wout_hbm.1, f32[6,1152]{1,0:T(8,128)} %mod.3, f32[1,1152]{1,0:T(1,128)} %reshape_tile.6.gain), custom_call_target="tpu_custom_call" | custom-call | flops 30000001024 | bytes 20000000 | tf_op jit(solution)/shard_map/spatial/pallas_call | solution.py:165
  84.2 8.6 %all-to-all-start.1 = ((bf16[64,8,1152]{2,1,0:T(8,128)(2,1)}), bf16[64,8,1152]{2,1,0:T(8,128)(2,1)S(1)}, u32[]{:S(2)}, u32[]{:S(2)}) async-start(bf16[64,8,1152]{2,1,0:T(8,128)(2,1)} %bitcast.50), calls=%async_computation.1 | async-start | bytes 2359296 | tf_op jit(solution)/shard_map/all_to_all | solution.py:410
  92.9 0.9 pad_maximum_fusion.2
  93.8 18.6 %all-to-all-done.1 = bf16[64,8,1152]{2,1,0:T(8,128)(2,1)S(1)} async-done(((bf16[64,8,1152]{2,1,0:T(8,128)(2,1)}), bf16[64,8,1152]{2,1,0:T(8,128)(2,1)S(1)}, u32[]{:S(2)}, u32[]{:S(2)}) %all-to-all-start.1) | async-done | bytes 1179680 | tf_op jit(solution)/shard_map/all_to_all | solution.py:410
  112.5 1.4 collective-permute-start.7
  114.3 2.2 %collective-permute-start.5 = (bf16[300,576]{0,1:T(8,128)(2,1)S(1)}, bf16[300,576]{0,1:T(8,128)(2,1)}, u32[]{:S(2)}, u32[]{:S(2)}) collective-permute-start(bf16[300,576]{0,1:T(8,128)(2,1)S(1)} %pad_maximum_fusion.4), channel_id=1, source_target_pairs={{0,4},{4,8},{8,12},{12,0},{1,5},{5,9},{9,13},{13,1},{2,6},{6,10},{... | collective-permute-start | bytes 1036808 | tf_op jit(solution)/shard_map/ppermute | solution.py:380
  116.5 28.3 %temporal.1 = bf16[512,1152]{1,0:T(8,128)(2,1)} custom-call(s32[3]{0:T(128)} %pad_add_fusion.place, bf16[32,2,80,1152]{3,2,1,0:T(8,128)(2,1)} %bitcast.56, bf16[512,1152]{1,0:T(8,128)(2,1)} %bitcast.46, f32[6,1152]{1,0:T(8,128)} %mod.3, f32[1,1152]{1,0:T(1,128)} %reshape_tile.7.gain), custom_call_target="tpu_custom_call" | custom-call | flops 20000000000 | bytes 20000000 | tf_op jit(solution)/shard_map/temporal/pallas_call | solution.py:273
  144.8 4.3 %all-to-all-start.2 = ((bf16[8,64,1152]{2,1,0:T(8,128)(2,1)}), bf16[8,64,1152]{2,1,0:T(8,128)(2,1)}, u32[]{:S(2)}, u32[]{:S(2)}) async-start(bf16[8,64,1152]{2,1,0:T(8,128)(2,1)} %bitcast.49), calls=%async_computation.2 | async-start | bytes 2359296 | tf_op jit(solution)/shard_map/all_to_all | solution.py:420
  149.1 1.4 pad_maximum_fusion
  151.7 0.8 copy.12
  152.6 0.9 pad_maximum_fusion.3.tk
  153.5 1.4 pad_convert_fusion.tvt
  154.9 9.5 %all-to-all-done.2 = bf16[8,64,1152]{2,1,0:T(8,128)(2,1)} async-done(((bf16[8,64,1152]{2,1,0:T(8,128)(2,1)}), bf16[8,64,1152]{2,1,0:T(8,128)(2,1)}, u32[]{:S(2)}, u32[]{:S(2)}) %all-to-all-start.2) | async-done | bytes 1179680 | tf_op jit(solution)/shard_map/all_to_all | solution.py:420
  164.4 15.8 %cross.1 = bf16[8,64,1152]{2,1,0:T(8,128)(2,1)} custom-call(s32[3]{0:T(128)} %pad_add_fusion.place, bf16[8,2,80,2304]{3,2,1,0:T(8,128)(2,1)} %bitcast.57, bf16[512,1152]{1,0:T(8,128)(2,1)} %bitcast.16.x, bf16[304,1152]{1,0:T(8,128)(2,1)} %pad_maximum_fusion.3.tk, f32[1152,304]{1,0:T(8,128)} %pad_convert_fusion.tvt), custom_call_target="tpu_custom_call" | custom-call | flops 20000000000 | bytes 20000000 | tf_op jit(solution)/shard_map/cross/pallas_call | solution.py:333
  (46 shorter events, 4.3 us)
Async XLA Ops:
  6.5 15.6 %copy-start = (bf16[300,1152]{1,0:T(8,128)(2,1)S(1)}, bf16[300,1152]{1,0:T(8,128)(2,1)}, u32[]{:S(2)}) copy-start(bf16[300,1152]{1,0:T(8,128)(2,1)} %param.11) | copy-start | bytes 2073604
  6.5 110.0 %all-gather.7.cloned.1.call-start = ((), (), s32[]{:S(2)}) async-start(), calls=%async_computation.4 | async-start | bytes 12165120 | tf_op jit(solution)/shard_map/all_gather | solution.py:400
  7.5 8.8 %collective-permute-start.4 = (bf16[80,1152]{1,0:T(8,128)(2,1)S(1)}, bf16[80,1152]{1,0:T(8,128)(2,1)S(1)}, u32[]{:S(2)}, u32[]{:S(2)}) collective-permute-start(bf16[80,1152]{1,0:T(8,128)(2,1)S(1)} %dynamic_slice.20), channel_id=1, source_target_pairs={{0,18},{18,0},{2,16},{16,2},{1,19},{19,1},{3,17},{17,3},{4,22},{22... | collective-permute-start | bytes 552968 | tf_op jit(solution)/shard_map/ppermute | solution.py:367
  12.6 9.5 %copy-start.3 = (bf16[1152,2,72]{0,2,1:T(8,128)(2,1)S(1)}, bf16[1152,2,72]{0,2,1:T(8,128)(2,1)}, u32[]{:S(2)}) copy-start(bf16[1152,2,72]{0,2,1:T(8,128)(2,1)} %param.17) | copy-start | bytes 995332
  17.1 5.5 %copy-start.4 = (f32[4,72]{1,0:T(4,128)S(1)}, f32[4,72]{1,0:T(4,128)}, u32[]{:S(2)}) copy-start(f32[4,72]{1,0:T(4,128)} %param.13) | copy-start | bytes 3460
  17.1 6.9 %copy-start.5 = (s32[64]{0:T(128)S(1)}, s32[64]{0:T(128)}, u32[]{:S(2)}) copy-start(s32[64]{0:T(128)} %param.10) | copy-start | bytes 772
  17.1 25.8 %all-to-all-start = ((bf16[8,64,1152]{2,1,0:T(8,128)(2,1)}), bf16[8,64,1152]{2,1,0:T(8,128)(2,1)S(1)}, u32[]{:S(2)}, u32[]{:S(2)}) async-start(bf16[8,64,1152]{2,1,0:T(8,128)(2,1)} %param.9), calls=%async_computation | async-start | bytes 2359296 | tf_op jit(solution)/shard_map/all_to_all | solution.py:391
  22.5 4.5 %collective-permute-start = (bf16[300,144]{0,1:T(8,128)(2,1)S(1)}, bf16[300,144]{0,1:T(8,128)(2,1)S(1)}, u32[]{:S(2)}, u32[]{:S(2)}) collective-permute-start(bf16[300,144]{0,1:T(8,128)(2,1)S(1)} %convolution_convert_fusion), channel_id=1, source_target_pairs={{0,1},{1,0},{2,3},{3,2},{4,5},{5,4},{6,7},{7,6},{8,9},{9,8},{10,11... | collective-permute-start | bytes 259208 | tf_op jit(solution)/shard_map/ppermute | solution.py:371
  43.0 4.0 %copy-start.2 = (bf16[8,64,1152]{2,1,0:T(8,128)(2,1)}, bf16[8,64,1152]{2,1,0:T(8,128)(2,1)S(1)}, u32[]{:S(2)}) copy-start(bf16[8,64,1152]{2,1,0:T(8,128)(2,1)S(1)} %all-to-all-done) | copy-start | bytes 3538948
  43.0 4.0 %collective-permute-start.1 = (bf16[512,1152]{1,0:T(8,128)(2,1)S(1)}, bf16[512,1152]{1,0:T(8,128)(2,1)}, u32[]{:S(2)}, u32[]{:S(2)}) collective-permute-start(bf16[512,1152]{1,0:T(8,128)(2,1)S(1)} %bitcast.47), channel_id=1, source_target_pairs={{0,1},{1,0},{2,3},{3,2},{4,5},{5,4},{6,7},{7,6},{8,9},{9,8},{10,11... | collective-permute-start | bytes 3538952 | tf_op jit(solution)/shard_map/ppermute | solution.py:371
  43.0 41.2 %collective-permute-start.2 = (bf16[300,288]{0,1:T(8,128)(2,1)S(1)}, bf16[300,288]{0,1:T(8,128)(2,1)S(1)}, u32[]{:S(2)}, u32[]{:S(2)}) collective-permute-start(bf16[300,288]{0,1:T(8,128)(2,1)S(1)} %pad_maximum_fusion.6), channel_id=1, source_target_pairs={{0,2},{2,0},{1,3},{3,1},{4,6},{6,4},{5,7},{7,5},{8,10},{10,8},{9,1... | collective-permute-start | bytes 518408 | tf_op jit(solution)/shard_map/ppermute | solution.py:405
  43.0 41.2 %collective-permute-start.3 = (bf16[80,2304]{1,0:T(8,128)(2,1)S(1)}, bf16[80,2304]{1,0:T(8,128)(2,1)S(1)}, u32[]{:S(2)}, u32[]{:S(2)}) collective-permute-start(bf16[80,2304]{1,0:T(8,128)(2,1)S(1)} %constant_dynamic-slice_fusion.4), channel_id=1, source_target_pairs={{0,18},{18,0},{2,16},{16,2},{1,19},{19,1},{3,17},{17,3},{4,22},{22... | collective-permute-start | bytes 1105928 | tf_op jit(solution)/shard_map/ppermute | solution.py:367
  84.2 28.2 %all-to-all-start.1 = ((bf16[64,8,1152]{2,1,0:T(8,128)(2,1)}), bf16[64,8,1152]{2,1,0:T(8,128)(2,1)S(1)}, u32[]{:S(2)}, u32[]{:S(2)}) async-start(bf16[64,8,1152]{2,1,0:T(8,128)(2,1)} %bitcast.50), calls=%async_computation.1 | async-start | bytes 2359296 | tf_op jit(solution)/shard_map/all_to_all | solution.py:410
  92.8 62.0 %all-gather.5.cloned.1.call-start = ((), (), s32[]{:S(2)}) async-start(), calls=%async_computation.3 | async-start | bytes 6635520 | tf_op jit(solution)/shard_map/all_gather | solution.py:413
  112.4 4.1 %copy-start.1 = (bf16[64,8,1152]{2,1,0:T(8,128)(2,1)}, bf16[64,8,1152]{2,1,0:T(8,128)(2,1)S(1)}, u32[]{:S(2)}) copy-start(bf16[64,8,1152]{2,1,0:T(8,128)(2,1)S(1)} %all-to-all-done.1) | copy-start | bytes 3538948
  112.5 32.2 %collective-permute-start.7 = (bf16[300,576]{0,1:T(8,128)(2,1)S(1)}, bf16[300,576]{0,1:T(8,128)(2,1)S(1)}, u32[]{:S(2)}, u32[]{:S(2)}) collective-permute-start(bf16[300,576]{0,1:T(8,128)(2,1)S(1)} %pad_maximum_fusion.4), channel_id=1, source_target_pairs={{0,12},{4,0},{8,4},{12,8},{1,13},{5,1},{9,5},{13,9},{2,14},{6,2},{... | collective-permute-start | bytes 1036808 | tf_op jit(solution)/shard_map/ppermute | solution.py:380
  114.0 30.8 %collective-permute-start.6 = (bf16[300,576]{0,1:T(8,128)(2,1)S(1)}, bf16[300,576]{0,1:T(8,128)(2,1)S(1)}, u32[]{:S(2)}, u32[]{:S(2)}) collective-permute-start(bf16[300,576]{0,1:T(8,128)(2,1)S(1)} %pad_maximum_fusion.4), channel_id=1, source_target_pairs={{0,8},{4,12},{8,0},{12,4},{1,9},{5,13},{9,1},{13,5},{2,10},{6,14},... | collective-permute-start | bytes 1036808 | tf_op jit(solution)/shard_map/ppermute | solution.py:380
  114.3 30.5 %collective-permute-start.5 = (bf16[300,576]{0,1:T(8,128)(2,1)S(1)}, bf16[300,576]{0,1:T(8,128)(2,1)}, u32[]{:S(2)}, u32[]{:S(2)}) collective-permute-start(bf16[300,576]{0,1:T(8,128)(2,1)S(1)} %pad_maximum_fusion.4), channel_id=1, source_target_pairs={{0,4},{4,8},{8,12},{12,0},{1,5},{5,9},{9,13},{13,1},{2,6},{6,10},{... | collective-permute-start | bytes 1036808 | tf_op jit(solution)/shard_map/ppermute | solution.py:380
  144.8 19.6 %all-to-all-start.2 = ((bf16[8,64,1152]{2,1,0:T(8,128)(2,1)}), bf16[8,64,1152]{2,1,0:T(8,128)(2,1)}, u32[]{:S(2)}, u32[]{:S(2)}) async-start(bf16[8,64,1152]{2,1,0:T(8,128)(2,1)} %bitcast.49), calls=%async_computation.2 | async-start | bytes 2359296 | tf_op jit(solution)/shard_map/all_to_all | solution.py:420
Sparse Core Ops, SparseCore 0:
  17.2 64.9 all-gather.6
  112.5 36.0 all-gather.4
